TPU v7x, 256 devices: a whole 4x4x8 slice. The times are simulated.
256 devices in a mesh: gx: 64 (over z, y, core), gy: 4 (over x).
Axes of the slice: x: 4, y: 4, z: 8, core: 2. Of those that a mesh axis runs over, the one named last changes fastest.
Arguments:
- velocity_u: float32 [16, 4096, 512], P(None, 'gx', 'gy'), may hold values from -6 to 6
- velocity_v: float32 [16, 4096, 512], P(None, 'gx', 'gy'), may hold values from -6 to 6
- velocity_w: float32 [16, 4096, 512], P(None, 'gx', 'gy'), may hold values from -6 to 6
- potential: float32 [16, 4096, 512], P(None, 'gx', 'gy'), may hold values from -6 to 6
Outputs:
- lorentz: float32 [3, 16, 4096, 512], P(None, None, 'gx', 'gy')
- vorticity: float32 [3, 16, 4096, 512], P(None, None, 'gx', 'gy')
- divergence: float32 [16, 4096, 512], P(None, 'gx', 'gy')
All inputs are finite; a program needn't handle non-finite values.
Results may differ from a plain program's by a relative error of at most 0.00005.
Values sent between devices are 32-bit elements; how exact they have to be, the bound alone decides.
No kernel may reach another device: no remote copies, remote signals or barrier semaphores. Data moves between devices by JAX's collectives and lax.ppermute only.
A program may use at most 128 MiB of HBM per device.

v0:
```python
import jax
import jax.numpy as jnp
from jax import lax
from jax.sharding import PartitionSpec as P

alpha_inner = 1.0 / 3.0
coef_near = 7.0 / 9.0
coef_far = 1.0 / 36.0
field_bx = 0.6
field_by = 0.8
highest = lax.Precision.HIGHEST


def extended(cells, sides, width):
    for axis, dim in sides:
        count = lax.axis_size(axis)
        ends = count - 1
        head = lax.slice_in_dim(cells, 0, width, axis=dim)
        tail = lax.slice_in_dim(cells, cells.shape[dim] - width, cells.shape[dim], axis=dim)
        cells = jnp.concatenate(
            [
                lax.ppermute(tail, axis, [(i, (i + 1) % count) for i in range(ends)]),
                cells,
                lax.ppermute(head, axis, [((i + 1) % count, i) for i in range(ends)]),
            ],
            axis=dim,
        )
    return cells


def z_derivative(field, axis):

    def plus(k):
        return jnp.roll(field, -k, axis) - jnp.roll(field, k, axis)

    return 0.75 * plus(1) - 0.15 * plus(2) + plus(3) / 60.0


def wall_coefficients(rows, total):
    edge = (rows == 1) | (rows == total - 2)
    lower = jnp.where(
        rows == 0, 0.0, jnp.where(edge, 0.25, jnp.where(rows == total - 1, 2.0, alpha_inner))
    )
    upper = jnp.where(
        rows == total - 1, 0.0, jnp.where(edge, 0.25, jnp.where(rows == 0, 2.0, alpha_inner))
    )
    return (lower.astype(jnp.float32), upper.astype(jnp.float32))


def block_inverse(lower, upper):
    count = lower.shape[0]
    lower = lower.at[0].set(0.0)
    upper = upper.at[count - 1].set(0.0)
    diagonal = jnp.ones((count,), jnp.float32)
    return lax.linalg.tridiagonal_solve(lower, diagonal, upper, jnp.eye(count, dtype=jnp.float32))


def join_blocks(solved, inverse, couplings, outer, dim):
    low_c, high_c, prev_w, next_v = couplings
    first = lax.index_in_dim(solved, 0, dim, keepdims=False)
    last = lax.index_in_dim(solved, solved.shape[dim] - 1, dim, keepdims=False)
    prev_last = outer[0].reshape(first.shape)
    next_first = outer[3].reshape(first.shape)
    v_first = low_c * inverse[0, 0]
    w_last = high_c * inverse[-1, -1]
    low_value = (prev_last - prev_w * first) / (1.0 - prev_w * v_first)
    high_value = (next_first - next_v * last) / (1.0 - next_v * w_last)
    shape_col = [1] * solved.ndim
    shape_col[dim] = -1
    v_col = (low_c * inverse[:, 0]).reshape(shape_col)
    w_col = (high_c * inverse[:, -1]).reshape(shape_col)
    return (
        solved - v_col * jnp.expand_dims(low_value, dim) - w_col * jnp.expand_dims(high_value, dim)
    )


def line_solve(right, block_len):
    batch, count, width = right.shape
    blocks = count // block_len
    constant = jnp.full((block_len,), alpha_inner, jnp.float32)
    inverse = block_inverse(constant, constant)
    pieces = right.reshape(batch, blocks, block_len, width)
    solved = jnp.einsum("ij,bnjc->bnic", inverse, pieces, precision=highest)
    first = solved[:, :, 0]
    last = solved[:, :, block_len - 1]
    prev_last = jnp.roll(last, 1, 1)
    next_first = jnp.roll(first, -1, 1)
    outer = [prev_last, prev_last, next_first, next_first]
    couplings = (
        alpha_inner,
        alpha_inner,
        alpha_inner * inverse[-1, -1],
        alpha_inner * inverse[0, 0],
    )
    joined = join_blocks(solved, inverse, couplings, outer, 2)
    return joined.reshape(batch, count, width)


def assemble(stacked, x_deriv, y_deriv, z_deriv):
    current_x = -x_deriv[3] - field_by * stacked[2]
    current_y = -y_deriv[3] + field_bx * stacked[2]
    current_z = -z_deriv[3] + field_by * stacked[0] - field_bx * stacked[1]
    lorentz = jnp.stack(
        [-field_by * current_z, field_bx * current_z, field_by * current_x - field_bx * current_y]
    )
    vorticity = jnp.stack(
        [y_deriv[2] - z_deriv[1], z_deriv[0] - x_deriv[2], x_deriv[1] - y_deriv[0]]
    )
    divergence = x_deriv[0] + y_deriv[1] + z_deriv[2]
    return (lorentz, vorticity, divergence)


def local(velocity_u, velocity_v, velocity_w, potential):
    stacked = jnp.stack([velocity_u, velocity_v, velocity_w, potential])
    depth, rows_x, rows_y = velocity_u.shape
    lines = lax.all_to_all(
        stacked.reshape(4 * depth, rows_x, rows_y), "gx", split_axis=0, concat_axis=1, tiled=True
    )
    right = coef_near * (jnp.roll(lines, -1, 1) - jnp.roll(lines, 1, 1)) + coef_far * (
        jnp.roll(lines, -2, 1) - jnp.roll(lines, 2, 1)
    )
    solved = line_solve(right, rows_x)
    x_deriv = lax.all_to_all(solved, "gx", split_axis=1, concat_axis=0, tiled=True).reshape(
        4, depth, rows_x, rows_y
    )
    padded_y = extended(stacked, (("gy", 3),), 2)
    right_y = coef_near * (padded_y[..., 3:-1] - padded_y[..., 1:-3]) + coef_far * (
        padded_y[..., 4:] - padded_y[..., :-4]
    )
    place = lax.axis_index("gy")
    count = lax.axis_size("gy")
    is_first = place == 0
    is_last = place == count - 1
    top = rows_y - 1
    right_y = right_y.at[..., 0].set(
        jnp.where(
            is_first,
            -2.5 * stacked[..., 0] + 2.0 * stacked[..., 1] + 0.5 * stacked[..., 2],
            right_y[..., 0],
        )
    )
    right_y = right_y.at[..., 1].set(
        jnp.where(is_first, 0.75 * (stacked[..., 2] - stacked[..., 0]), right_y[..., 1])
    )
    right_y = right_y.at[..., top - 1].set(
        jnp.where(
            is_last, 0.75 * (stacked[..., top] - stacked[..., top - 2]), right_y[..., top - 1]
        )
    )
    right_y = right_y.at[..., top].set(
        jnp.where(
            is_last,
            2.5 * stacked[..., top] - 2.0 * stacked[..., top - 1] - 0.5 * stacked[..., top - 2],
            right_y[..., top],
        )
    )
    total = rows_y * count
    start = place * rows_y
    offsets = jnp.arange(rows_y, dtype=jnp.int32)
    lower, upper = wall_coefficients(start + offsets, total)
    inverse_y = block_inverse(lower, upper)
    lower_prev, upper_prev = wall_coefficients(start - rows_y + offsets, total)
    lower_next, upper_next = wall_coefficients(start + rows_y + offsets, total)
    prev_w = upper_prev[-1] * block_inverse(lower_prev, upper_prev)[-1, -1]
    next_v = lower_next[0] * block_inverse(lower_next, upper_next)[0, 0]
    couplings_y = (lower[0], upper[-1], prev_w, next_v)
    solved_y = jnp.einsum("ij,fzxj->fzxi", inverse_y, right_y, precision=highest)
    edges_y = jnp.stack([solved_y[..., 0], solved_y[..., top]]).reshape(2, -1)
    outer_y = extended(edges_y, (("gy", 0),), 1)
    y_deriv = join_blocks(solved_y, inverse_y, couplings_y, outer_y, 3)
    z_deriv = z_derivative(stacked, 1)
    lorentz, vorticity, divergence = assemble(stacked, x_deriv, y_deriv, z_deriv)
    return (lorentz, vorticity, divergence)


def solution(mesh):
    in_specs = (P(None, "gx", "gy"), P(None, "gx", "gy"), P(None, "gx", "gy"), P(None, "gx", "gy"))
    out_specs = (P(None, None, "gx", "gy"), P(None, None, "gx", "gy"), P(None, "gx", "gy"))
    return jax.shard_map(local, mesh=mesh, in_specs=in_specs, out_specs=out_specs, check_vma=False)
```

profile of v0, /device:TPU:1, one launch (start us, length us, event | category | flops | bytes accessed | tf_op | source)
XLA Modules:
  0.0 1317.9 jit_solution(5760395238370865820)
XLA Ops:
  38.3 198.0 %while.120 = (s32[]{:T(128)}, f32[]{:T(128)}, f32[128]{0:T(128)S(1)}, f32[3,32]{1,0:T(4,128)S(1)}, f32[3,32,128]{2,1,0:T(8,128)S(1)}, /*index=5*/f32[3,32]{1,0:T...) while((s32[]{:T(128)}, f32[]{:T(128)}, ...), condition=%wide.region_1.2_spmd, body=%wide.region_0.1_spmd.sunk | while | flops 12417 | bytes 103653 | solution.py:55
  81.7 20.6 %fusion.1007 = (f32[128]{0:T(128)S(1)}, f32[128]{0:T(128)S(1)}, f32[128]{0:T(128)S(1)}, f32[128]{0:T(128)S(1)}, f32[128]{0:T(128)S(1)}, /*index=5*/f32[128]{0:T(...) fusion(f32[3,32,128]{2,1,0:T(8,128)S(1)} %get-tuple-element.293, ...), kind=kLoop, calls=%fused_computation.40.clone.1 | loop fusion | flops 12288 | bytes 33664 | tf_op jit(solution)/shard_map/while/body/eval_jaxpr/div | solution.py:55
  147.7 20.6 %fusion.1007 = (f32[128]{0:T(128)S(1)}, f32[128]{0:T(128)S(1)}, f32[128]{0:T(128)S(1)}, f32[128]{0:T(128)S(1)}, f32[128]{0:T(128)S(1)}, /*index=5*/f32[128]{0:T(...) fusion(f32[3,32,128]{2,1,0:T(8,128)S(1)} %get-tuple-element.293, ...), kind=kLoop, calls=%fused_computation.40.clone.1 | loop fusion | flops 12288 | bytes 33664 | tf_op jit(solution)/shard_map/while/body/eval_jaxpr/div | solution.py:55
  213.7 20.6 %fusion.1007 = (f32[128]{0:T(128)S(1)}, f32[128]{0:T(128)S(1)}, f32[128]{0:T(128)S(1)}, f32[128]{0:T(128)S(1)}, f32[128]{0:T(128)S(1)}, /*index=5*/f32[128]{0:T(...) fusion(f32[3,32,128]{2,1,0:T(8,128)S(1)} %get-tuple-element.293, ...), kind=kLoop, calls=%fused_computation.40.clone.1 | loop fusion | flops 12288 | bytes 33664 | tf_op jit(solution)/shard_map/while/body/eval_jaxpr/div | solution.py:55
  263.1 211.8 %while.122 = (s32[]{:T(128)}, f32[]{:T(128)}, f32[128]{0:T(128)S(1)}, f32[3,32]{1,0:T(4,128)}, f32[3,32,128]{2,1,0:T(8,128)}, /*index=5*/f32[3,32]{1,0:T(4,128)}...) while((s32[]{:T(128)}, f32[]{:T(128)}, ...), condition=%wide.region_5.6_spmd, body=%wide.region_4.5_spmd.sunk | while | flops 12417 | bytes 104161 | solution.py:55
  306.4 20.9 %fusion.1015 = (f32[128]{0:T(128)}, f32[128]{0:T(128)S(1)}, f32[128]{0:T(128)S(1)}, f32[128]{0:T(128)S(1)}, f32[128]{0:T(128)S(1)}, /*index=5*/f32[128]{0:T(128)...) fusion(f32[3,32,128]{2,1,0:T(8,128)S(1)} %get-tuple-element.341, ...), kind=kLoop, calls=%fused_computation.269.clone.1 | loop fusion | flops 12288 | bytes 33664 | tf_op jit(solution)/shard_map/while/body/eval_jaxpr/div | solution.py:55
  377.0 20.9 %fusion.1015 = (f32[128]{0:T(128)}, f32[128]{0:T(128)S(1)}, f32[128]{0:T(128)S(1)}, f32[128]{0:T(128)S(1)}, f32[128]{0:T(128)S(1)}, /*index=5*/f32[128]{0:T(128)...) fusion(f32[3,32,128]{2,1,0:T(8,128)S(1)} %get-tuple-element.341, ...), kind=kLoop, calls=%fused_computation.269.clone.1 | loop fusion | flops 12288 | bytes 33664 | tf_op jit(solution)/shard_map/while/body/eval_jaxpr/div | solution.py:55
  447.6 20.9 %fusion.1015 = (f32[128]{0:T(128)}, f32[128]{0:T(128)S(1)}, f32[128]{0:T(128)S(1)}, f32[128]{0:T(128)S(1)}, f32[128]{0:T(128)S(1)}, /*index=5*/f32[128]{0:T(128)...) fusion(f32[3,32,128]{2,1,0:T(8,128)S(1)} %get-tuple-element.341, ...), kind=kLoop, calls=%fused_computation.269.clone.1 | loop fusion | flops 12288 | bytes 33664 | tf_op jit(solution)/shard_map/while/body/eval_jaxpr/div | solution.py:55
  552.2 21.0 %subtract_divide_fusion.62 = (f32[128]{0:T(128)S(1)}, f32[128]{0:T(128)S(1)}, f32[128]{0:T(128)S(1)}, f32[128]{0:T(128)S(1)}, f32[128]{0:T(128)S(1)}, /*index=5*...) fusion(f32[]{:T(128)S(6)} %sub.21948, ...), kind=kLoop, calls=%fused_computation.1197 | loop fusion | flops 11904 | bytes 32504 | tf_op jit(solution)/shard_map/eval_jaxpr/div | solution.py:55
  582.7 81.3 %while.121 = (s32[]{:T(128)}, f32[128]{0:T(128)S(1)}, f32[3,32,128]{2,1,0:T(8,128)}, f32[3,32,128]{2,1,0:T(8,128)}, f32[3,32]{1,0:T(4,128)}, /*index=5*/s32[]{:T...) while((s32[]{:T(128)}, f32[128]{0:T(128)S(1)}, ...), condition=%wide.region_3.4_spmd, body=%wide.region_2.3_spmd.sunk | while | flops 8226 | bytes 101333 | solution.py:55
  584.8 21.6 %fusion.1010 = (f32[128]{0:T(128)}, f32[128]{0:T(128)S(1)}, f32[128]{0:T(128)S(1)}, f32[128]{0:T(128)S(1)}, f32[128]{0:T(128)S(1)}, /*index=5*/f32[128]{0:T(128)...) fusion(f32[3,32,128]{2,1,0:T(8,128)} %get-tuple-element.3052, ...), kind=kLoop, calls=%fused_computation.168.clone.1 | loop fusion | flops 8192 | bytes 33536 | tf_op jit(solution)/shard_map/while/body/eval_jaxpr/sub | solution.py:55
  611.9 21.6 %fusion.1010 = (f32[128]{0:T(128)}, f32[128]{0:T(128)S(1)}, f32[128]{0:T(128)S(1)}, f32[128]{0:T(128)S(1)}, f32[128]{0:T(128)S(1)}, /*index=5*/f32[128]{0:T(128)...) fusion(f32[3,32,128]{2,1,0:T(8,128)} %get-tuple-element.3052, ...), kind=kLoop, calls=%fused_computation.168.clone.1 | loop fusion | flops 8192 | bytes 33536 | tf_op jit(solution)/shard_map/while/body/eval_jaxpr/sub | solution.py:55
  639.0 21.6 %fusion.1010 = (f32[128]{0:T(128)}, f32[128]{0:T(128)S(1)}, f32[128]{0:T(128)S(1)}, f32[128]{0:T(128)S(1)}, f32[128]{0:T(128)S(1)}, /*index=5*/f32[128]{0:T(128)...) fusion(f32[3,32,128]{2,1,0:T(8,128)} %get-tuple-element.3052, ...), kind=kLoop, calls=%fused_computation.168.clone.1 | loop fusion | flops 8192 | bytes 33536 | tf_op jit(solution)/shard_map/while/body/eval_jaxpr/sub | solution.py:55
  667.8 214.4 %while.124 = (s32[]{:T(128)}, f32[]{:T(128)}, f32[128]{0:T(128)S(1)}, f32[3,32]{1,0:T(4,128)}, f32[3,32,128]{2,1,0:T(8,128)}, /*index=5*/f32[3,32]{1,0:T(4,128)}...) while((s32[]{:T(128)}, f32[]{:T(128)}, ...), condition=%wide.region_9.10_spmd, body=%wide.region_8.9_spmd.sunk | while | flops 12417 | bytes 104161 | solution.py:55
  711.3 21.2 %fusion.1023 = (f32[128]{0:T(128)}, f32[128]{0:T(128)S(1)}, f32[128]{0:T(128)S(1)}, f32[128]{0:T(128)S(1)}, f32[128]{0:T(128)S(1)}, /*index=5*/f32[128]{0:T(128)...) fusion(f32[3,32,128]{2,1,0:T(8,128)S(1)} %get-tuple-element.317, ...), kind=kLoop, calls=%fused_computation.498.clone.1 | loop fusion | flops 12288 | bytes 33664 | tf_op jit(solution)/shard_map/while/body/eval_jaxpr/div | solution.py:55
  782.6 21.2 %fusion.1023 = (f32[128]{0:T(128)}, f32[128]{0:T(128)S(1)}, f32[128]{0:T(128)S(1)}, f32[128]{0:T(128)S(1)}, f32[128]{0:T(128)S(1)}, /*index=5*/f32[128]{0:T(128)...) fusion(f32[3,32,128]{2,1,0:T(8,128)S(1)} %get-tuple-element.317, ...), kind=kLoop, calls=%fused_computation.498.clone.1 | loop fusion | flops 12288 | bytes 33664 | tf_op jit(solution)/shard_map/while/body/eval_jaxpr/div | solution.py:55
  854.0 21.2 %fusion.1023 = (f32[128]{0:T(128)}, f32[128]{0:T(128)S(1)}, f32[128]{0:T(128)S(1)}, f32[128]{0:T(128)S(1)}, f32[128]{0:T(128)S(1)}, /*index=5*/f32[128]{0:T(128)...) fusion(f32[3,32,128]{2,1,0:T(8,128)S(1)} %get-tuple-element.317, ...), kind=kLoop, calls=%fused_computation.498.clone.1 | loop fusion | flops 12288 | bytes 33664 | tf_op jit(solution)/shard_map/while/body/eval_jaxpr/div | solution.py:55
  943.0 21.1 %subtract_divide_fusion.31 = (f32[128]{0:T(128)S(1)}, f32[128]{0:T(128)}, f32[128]{0:T(128)}, f32[128]{0:T(128)}, f32[128]{0:T(128)}, /*index=5*/f32[128]{0:T(12...) fusion(f32[]{:T(128)S(6)} %sub.22042, ...), kind=kLoop, calls=%fused_computation.1165 | loop fusion | flops 11904 | bytes 32504 | tf_op jit(solution)/shard_map/eval_jaxpr/div | solution.py:55
  1013.6 21.2 %subtract_divide_fusion = (f32[128]{0:T(128)S(1)}, f32[128]{0:T(128)}, f32[128]{0:T(128)}, f32[128]{0:T(128)}, f32[128]{0:T(128)}, /*index=5*/f32[128]{0:T(128)}...) fusion(f32[]{:T(128)S(6)} %sub.22107, ...), kind=kLoop, calls=%fused_computation.1133 | loop fusion | flops 11904 | bytes 32504 | tf_op jit(solution)/shard_map/eval_jaxpr/div | solution.py:55
  1054.1 65.6 %while.125 = (s32[]{:T(128)}, f32[128]{0:T(128)S(1)}, f32[3,32,128]{2,1,0:T(8,128)S(1)}, f32[3,32]{1,0:T(4,128)S(1)}, s32[]{:T(128)}, /*index=5*/s32[]{:T(128)},...) while((s32[]{:T(128)}, f32[128]{0:T(128)S(1)}, ...), condition=%wide.region_11.12_spmd, body=%wide.region_10.11_spmd.sunk | while | flops 8226 | bytes 18889 | solution.py:55
  1055.5 20.4 %fusion.1026 = f32[128]{0:T(128)S(1)} fusion(f32[3,32,128]{2,1,0:T(8,128)S(1)} %get-tuple-element.3292, s32[]{:T(128)S(6)} %sub.24736, s32[]{:T(128)S(6)} %add.795, s32[]{:T(128)S(6)} %add.796, s32[]{:T(128)S(6)} %add.797, s32[]{:T(128)S(6)} %add.798, s32[]{:T(128)S(6)} %add.799, s32[]{:T(128)S(6)} %add.800, s32[]{:T(128)S(6)} %add.801, ...), kind=kLoop, calls=%fused_computation.627.clone.1 | loop fusion | flops 8192 | bytes 17664 | tf_op jit(solution)/shard_map/while/body/eval_jaxpr/sub | solution.py:55
  1077.4 20.4 %fusion.1026 = f32[128]{0:T(128)S(1)} fusion(f32[3,32,128]{2,1,0:T(8,128)S(1)} %get-tuple-element.3292, s32[]{:T(128)S(6)} %sub.24736, s32[]{:T(128)S(6)} %add.795, s32[]{:T(128)S(6)} %add.796, s32[]{:T(128)S(6)} %add.797, s32[]{:T(128)S(6)} %add.798, s32[]{:T(128)S(6)} %add.799, s32[]{:T(128)S(6)} %add.800, s32[]{:T(128)S(6)} %add.801, ...), kind=kLoop, calls=%fused_computation.627.clone.1 | loop fusion | flops 8192 | bytes 17664 | tf_op jit(solution)/shard_map/while/body/eval_jaxpr/sub | solution.py:55
  1099.2 20.4 %fusion.1026 = f32[128]{0:T(128)S(1)} fusion(f32[3,32,128]{2,1,0:T(8,128)S(1)} %get-tuple-element.3292, s32[]{:T(128)S(6)} %sub.24736, s32[]{:T(128)S(6)} %add.795, s32[]{:T(128)S(6)} %add.796, s32[]{:T(128)S(6)} %add.797, s32[]{:T(128)S(6)} %add.798, s32[]{:T(128)S(6)} %add.799, s32[]{:T(128)S(6)} %add.800, s32[]{:T(128)S(6)} %add.801, ...), kind=kLoop, calls=%fused_computation.627.clone.1 | loop fusion | flops 8192 | bytes 17664 | tf_op jit(solution)/shard_map/while/body/eval_jaxpr/sub | solution.py:55
  1119.6 65.9 %while.123 = (s32[]{:T(128)}, f32[128]{0:T(128)S(1)}, f32[3,32,128]{2,1,0:T(8,128)S(1)}, f32[3,32,128]{2,1,0:T(8,128)S(1)}, f32[3,32]{1,0:T(4,128)S(1)}, /*index...) while((s32[]{:T(128)}, f32[128]{0:T(128)S(1)}, ...), condition=%wide.region_7.8_spmd, body=%wide.region_6.7_spmd.sunk | while | flops 8226 | bytes 101333 | solution.py:55
  (430 shorter events, 443.7 us)
Async XLA Ops:
  11.0 1210.9 %collective-permute-start = (f32[4,16,64,2]{2,1,3,0:T(8,128)}, f32[4,16,64,2]{2,1,3,0:T(8,128)}, u32[]{:S(2)}, u32[]{:S(2)}) collective-permute-start(f32[4,16,64,2]{2,1,3,0:T(8,128)} %copy.33), channel_id=1, source_target_pairs={{1,0},{2,1},{3,2},{5,4},{6,5},{7,6},{9,8},{10,9},{11,10},{13,12},{... | collective-permute-start | bytes 98312 | tf_op jit(solution)/shard_map/ppermute | solution.py:24
  13.6 1209.9 %collective-permute-start.1 = (f32[4,16,64,2]{2,1,3,0:T(8,128)}, f32[4,16,64,2]{2,1,3,0:T(8,128)}, u32[]{:S(2)}, u32[]{:S(2)}) collective-permute-start(f32[4,16,64,2]{2,1,3,0:T(8,128)} %copy.35), channel_id=1, source_target_pairs={{0,1},{1,2},{2,3},{4,5},{5,6},{6,7},{8,9},{9,10},{10,11},{12,13},{... | collective-permute-start | bytes 98312 | tf_op jit(solution)/shard_map/ppermute | solution.py:22
  18.8 1166.8 %all-to-all-start = ((f32[64,64,128]{2,1,0:T(8,128)}), f32[64,64,128]{2,1,0:T(8,128)S(1)}, u32[]{:S(2)}, u32[]{:S(2)}) async-start(f32[64,64,128]{2,1,0:T(8,128)} %bitcast.751), calls=%async_computation | async-start | bytes 4194304 | tf_op jit(solution)/shard_map/all_to_all | solution.py:116
  474.9 77.3 %copy-start.13 = (f32[128]{0:T(128)}, f32[128]{0:T(128)S(1)}, u32[]{:S(2)}) copy-start(f32[128]{0:T(128)S(1)} %get-tuple-element.631) | copy-start | bytes 1540
  573.3 94.5 %copy-start.12 = (f32[128]{0:T(128)S(1)}, f32[128]{0:T(128)}, u32[]{:S(2)}) copy-start(f32[128]{0:T(128)} %copy-done.11) | copy-start | bytes 1540
  667.8 275.2 %copy-start.14 = (f32[128]{0:T(128)S(1)}, f32[128]{0:T(128)}, u32[]{:S(2)}) copy-start(f32[128]{0:T(128)} %copy-done.13) | copy-start | bytes 1540
  969.7 43.9 %copy-start.17 = (f32[128]{0:T(128)}, f32[128]{0:T(128)S(1)}, u32[]{:S(2)}) copy-start(f32[128]{0:T(128)S(1)} %get-tuple-element.1050) | copy-start | bytes 1540
  972.9 61.9 %copy-start.19 = (f32[128]{0:T(128)}, f32[128]{0:T(128)S(1)}, u32[]{:S(2)}) copy-start(f32[128]{0:T(128)S(1)} %get-tuple-element.1052) | copy-start | bytes 1540
  976.1 64.8 %copy-start.21 = (f32[128]{0:T(128)}, f32[128]{0:T(128)S(1)}, u32[]{:S(2)}) copy-start(f32[128]{0:T(128)S(1)} %get-tuple-element.1054) | copy-start | bytes 1540
  979.3 61.6 %copy-start.23 = (f32[128]{0:T(128)}, f32[128]{0:T(128)S(1)}, u32[]{:S(2)}) copy-start(f32[128]{0:T(128)S(1)} %get-tuple-element.1056) | copy-start | bytes 1540
  982.5 58.4 %copy-start.25 = (f32[128]{0:T(128)}, f32[128]{0:T(128)S(1)}, u32[]{:S(2)}) copy-start(f32[128]{0:T(128)S(1)} %get-tuple-element.1058) | copy-start | bytes 1540
  985.6 55.3 %copy-start.27 = (f32[128]{0:T(128)}, f32[128]{0:T(128)S(1)}, u32[]{:S(2)}) copy-start(f32[128]{0:T(128)S(1)} %get-tuple-element.1060) | copy-start | bytes 1540
  988.8 52.1 %copy-start.29 = (f32[128]{0:T(128)}, f32[128]{0:T(128)S(1)}, u32[]{:S(2)}) copy-start(f32[128]{0:T(128)S(1)} %get-tuple-element.1062) | copy-start | bytes 1540
  991.9 49.0 %copy-start.31 = (f32[128]{0:T(128)}, f32[128]{0:T(128)S(1)}, u32[]{:S(2)}) copy-start(f32[128]{0:T(128)S(1)} %get-tuple-element.1064) | copy-start | bytes 1540
  995.1 45.9 %copy-start.33 = (f32[128]{0:T(128)}, f32[128]{0:T(128)S(1)}, u32[]{:S(2)}) copy-start(f32[128]{0:T(128)S(1)} %get-tuple-element.1066) | copy-start | bytes 1540
  998.3 42.7 %copy-start.35 = (f32[128]{0:T(128)}, f32[128]{0:T(128)S(1)}, u32[]{:S(2)}) copy-start(f32[128]{0:T(128)S(1)} %get-tuple-element.1068) | copy-start | bytes 1540
  1001.4 33.4 %copy-start.37 = (f32[128]{0:T(128)}, f32[128]{0:T(128)S(1)}, u32[]{:S(2)}) copy-start(f32[128]{0:T(128)S(1)} %get-tuple-element.1070) | copy-start | bytes 1540
  1191.0 30.5 %copy-start.24 = (f32[128]{0:T(128)S(1)}, f32[128]{0:T(128)}, u32[]{:S(2)}) copy-start(f32[128]{0:T(128)} %copy-done.23) | copy-start | bytes 1540
  1191.0 30.5 %copy-start.26 = (f32[128]{0:T(128)S(1)}, f32[128]{0:T(128)}, u32[]{:S(2)}) copy-start(f32[128]{0:T(128)} %copy-done.25) | copy-start | bytes 1540
  1191.0 30.5 %copy-start.28 = (f32[128]{0:T(128)S(1)}, f32[128]{0:T(128)}, u32[]{:S(2)}) copy-start(f32[128]{0:T(128)} %copy-done.27) | copy-start | bytes 1540
  1191.0 30.5 %copy-start.30 = (f32[128]{0:T(128)S(1)}, f32[128]{0:T(128)}, u32[]{:S(2)}) copy-start(f32[128]{0:T(128)} %copy-done.29) | copy-start | bytes 1540
  1191.3 117.5 %all-to-all-start.1 = ((f32[1,4096,128]{2,0,1:T(1,128)}), f32[1,4096,128]{2,0,1:T(1,128)}, u32[]{:S(2)}, u32[]{:S(2)}) async-start(f32[1,4096,128]{2,0,1:T(1,128)} %bitcast.5060), calls=%async_computation.1 | async-start | bytes 4194304 | tf_op jit(solution)/shard_map/all_to_all | solution.py:123
  1291.8 12.6 collective-permute-start.2
  1296.7 9.0 collective-permute-start.3
  (45 other events, 999.6 us)
where the time goes:
time: 1340 us; the launch traced here: 1320 us
  other arithmetic  574 us (43%)
  loops' own time  372 us (28%)
  local copies, waits for them, and re-layouts  209 us (16%)
  between operations  125 us (9%)
  starting transfers between devices  34.3 us (3%)
    another operation x6, loops' own time, block_inverse(): lax.linalg.tridiagonal_solve(lower, diagonal, upper, jnp.eye(count, dtype...  372 us
    div x13, other arithmetic, block_inverse(): lax.linalg.tridiagonal_solve(lower, diagonal, upper, jnp.eye(count, dtype...  252 us
    sub x10, other arithmetic, block_inverse(): lax.linalg.tridiagonal_solve(lower, diagonal, upper, jnp.eye(count, dtype...  189 us
    broadcast_in_dim x28, other arithmetic, block_inverse(): lax.linalg.tridiagonal_solve(lower, diagonal, upper, jnp.eye(count, dtype...  81.8 us
    slice x81, local copies, waits for them, and re-layouts, block_inverse(): lax.linalg.tridiagonal_solve(lower, diagonal, upper, jnp.eye(count, dtype...  51.6 us
    concatenate x32, local copies, waits for them, and re-layouts, block_inverse(): lax.linalg.tridiagonal_solve(lower, diagonal, upper, jnp.eye(count, dtype...  47 us
  transfers between devices with their start and end apart: 6, of which 0 were waited for; matrix products, arithmetic and copies ran while one was open for 58% of the time, Pallas kernels for 0%

commit v1 on v0

v1 whole, which is shorter than its diff:
```python
import functools
import math

import jax
import jax.numpy as jnp
import ml_dtypes
import numpy as np
from jax import lax
from jax.experimental import pallas as pl
from jax.experimental.pallas import tpu as pltpu
from jax.sharding import PartitionSpec as P

third = 1.0 / 3.0
near = 7.0 / 9.0
far = 1.0 / 36.0
bx = 0.6
by = 0.8

lam = (-3.0 + math.sqrt(5.0)) / 2.0
scale = 1.0 / (1.0 + 2.0 * third * lam)
log_lam = math.log(-lam)
gamma = scale * (near * (lam - 1.0 / lam) + far * (lam**2 - lam**-2))
edge = scale * (near * (lam**2 - 1.0) + far * (lam**3 - lam)) - gamma * lam

f32 = jnp.float32
bf16 = jnp.bfloat16


def halves(values):
    high = values.astype(bf16)
    return high, (values - high.astype(f32)).astype(bf16)


def host_halves(values):
    values = values.astype(np.float32)
    high = values.astype(ml_dtypes.bfloat16)
    low = (values - high.astype(np.float32)).astype(ml_dtypes.bfloat16)
    return high, low


def x_operator(count):
    h = lambda m: scale * lam ** np.abs(m)
    i = np.arange(count)
    m = i[:, None] - i[None, :]
    own = near * (h(m + 1) - h(m - 1)) + far * (h(m + 2) - h(m - 2))
    high, low = host_halves(own)
    return np.concatenate([high, low, high], axis=1)


def y_operators(total, blocks):
    a = np.eye(total)
    b = np.zeros((total, total))
    for j in range(2, total - 2):
        a[j, j - 1] = a[j, j + 1] = third
        b[j, j + 1], b[j, j - 1], b[j, j + 2], b[j, j - 2] = near, -near, far, -far
    a[0, 1] = a[-1, -2] = 2.0
    b[0, :3] = -2.5, 2.0, 0.5
    b[-1, -3:] = -0.5, -2.0, 2.5
    for j in (1, total - 2):
        a[j, j - 1] = a[j, j + 1] = 0.25
        b[j, j + 1], b[j, j - 1] = 0.75, -0.75
    whole = np.linalg.solve(a, b)
    size = total // blocks
    out = []
    for g in range(blocks):
        own = whole[g * size : (g + 1) * size, g * size : (g + 1) * size].T
        high, low = host_halves(own)
        out.append(np.block([[high, low], [high, np.zeros_like(low)]]))
    return np.stack(out)


def power(n):
    size = jnp.exp(n.astype(f32) * log_lam)
    return jnp.where((n & 1) == 0, size, -size)


def edges_kernel(u, v, w, p, fields, msg_a, msg_b, msg_c, msg_d, sems):
    sources = (u, v, w, p)
    copies = [pltpu.make_async_copy(s, fields.at[i], sems.at[i]) for i, s in enumerate(sources)]
    for c in copies:
        c.start()
    depth, rows, lanes = u.shape
    even_x = lax.rem(lax.axis_index("gx"), 2) == 0
    even_y = lax.rem(lax.axis_index("gy"), 2) == 0

    k = lax.broadcasted_iota(jnp.int32, (rows, lanes), 0)
    to_right = gamma * power(rows - k)
    to_left = -gamma * power(k + 1)
    weights_a = jnp.where(even_x, to_right, to_left)
    weights_b = jnp.where(even_x, to_left, to_right)

    j = lax.broadcasted_iota(jnp.int32, (8, lanes), 1)
    row = lax.broadcasted_iota(jnp.int32, (8, lanes), 0)
    y_right = jnp.where((row & 1) == 0, gamma * power(lanes - j), jnp.where(j == lanes - 1, edge, 0.0))
    y_left = jnp.where((row & 1) == 0, -gamma * power(j + 1), jnp.where(j == 0, -edge, 0.0))
    rightward = (row < 2) == even_y
    high, low = halves(jnp.where(rightward, y_right, y_left))
    both = jnp.concatenate([high, low], axis=0)

    for i in range(4):
        copies[i].wait()
        f = fields[i]
        first, last = f[:, 0, :], f[:, rows - 1, :]
        rr, ll = edge * last, -edge * first
        msg_a[pl.ds(2 * i * depth, depth), :] = jnp.sum(f * weights_a[None], axis=1)
        msg_a[pl.ds((2 * i + 1) * depth, depth), :] = jnp.where(even_x, rr, ll)
        msg_b[pl.ds(2 * i * depth, depth), :] = jnp.sum(f * weights_b[None], axis=1)
        msg_b[pl.ds((2 * i + 1) * depth, depth), :] = jnp.where(even_x, ll, rr)
    nt = (((1,), (1,)), ((), ()))
    for i in range(4):
        fh, fl = halves(fields[i].reshape(depth * rows, lanes))
        top = lax.dot_general(both, fh, nt, preferred_element_type=f32)
        rest = lax.dot_general(both, fl, nt, preferred_element_type=f32)
        sums = top[0:8] + top[8:16] + rest[0:8]
        msg_c[pl.ds(2 * i, 2), :] = sums[0:2]
        msg_d[pl.ds(2 * i, 2), :] = sums[2:4]


def local_kernel(fields, wx, wy_all, lorentz, lz_o, vx_o, vy_o, vz_o, dv_o, wy, lx_s, ly_s, sems):
    gy = lax.axis_index("gy")
    get = pltpu.make_async_copy(wy_all.at[gy], wy, sems.at[0])
    get.start()
    _, depth, rows, lanes = fields.shape
    u, v, w, p = range(4)

    def dz(i, k):
        at = lambda s: fields[i, (k + s) % depth]
        return (
            0.75 * (at(1) - at(-1)) - 0.15 * (at(2) - at(-2)) + (1.0 / 60.0) * (at(3) - at(-3))
        )

    for k in range(depth):
        jz = by * fields[u, k] - bx * fields[v, k] - dz(p, k)
        lx_s[k] = -by * jz
        ly_s[k] = bx * jz
    put_x = pltpu.make_async_copy(lx_s, lorentz.at[0], sems.at[1])
    put_y = pltpu.make_async_copy(ly_s, lorentz.at[1], sems.at[2])
    put_x.start()
    put_y.start()
    get.wait()
    for k in range(depth):
        split = [halves(fields[i, k]) for i in range(4)]
        highs = jnp.concatenate([s[0] for s in split], axis=0)
        lows = jnp.concatenate([s[1] for s in split], axis=0)
        y = jnp.dot(
            jnp.concatenate([highs, lows], axis=1), wy[...], preferred_element_type=f32
        )
        y = y[:, :lanes] + y[:, lanes:]
        wide_h = jnp.concatenate([s[0] for s in split], axis=1)
        wide_l = jnp.concatenate([s[1] for s in split], axis=1)
        x = jnp.dot(
            wx[...], jnp.concatenate([wide_h, wide_h, wide_l], axis=0), preferred_element_type=f32
        )
        yd = lambda i: y[i * rows : (i + 1) * rows]
        xd = lambda i: x[:, i * lanes : (i + 1) * lanes]
        lz_o[k] = bx * yd(p) - by * xd(p) - fields[w, k]
        vx_o[k] = yd(w) - dz(v, k)
        vy_o[k] = dz(u, k) - xd(w)
        vz_o[k] = xd(v) - yd(u)
        dv_o[k] = xd(u) + yd(v) + dz(w, k)
    put_x.wait()
    put_y.wait()


def join_kernel(
    got_a, got_b, got_c, got_d, lz, vx, vy, vz, dv, lorentz_in, lorentz, vorticity, divergence,
    lz_s, vx_s, vy_s, vz_s, dv_s, sems
):
    depth, rows, lanes = lz.shape
    gy, blocks = lax.axis_index("gy"), lax.axis_size("gy")
    even_x = lax.rem(lax.axis_index("gx"), 2) == 0
    even_y = lax.rem(gy, 2) == 0
    inner = jnp.logical_and(gy > 0, gy < blocks - 1)

    width = 4 * lanes
    lane = lax.broadcasted_iota(jnp.int32, (16, width), 1)
    row = lax.broadcasted_iota(jnp.int32, (16, width), 0)
    j = lane & (lanes - 1)
    left = jnp.where((row & 1) == 0, power(j), jnp.where(j == 0, 1.0, 0.0))
    right = jnp.where((row & 1) == 0, power(lanes - 1 - j), jnp.where(j == lanes - 1, 1.0, 0.0))
    from_d = row >= 8
    spread = jnp.where(from_d == even_y, left, right)
    field = (row & 7) >> 1
    target = lane // lanes
    hit = jnp.where(field == 0, 2, jnp.where(field == 1, 3, jnp.where(field == 2, 1, 0))) == target
    factor = jnp.where(target == 0, bx, jnp.where(target == 2, -1.0, 1.0))
    spread = jnp.where(hit, spread * factor, 0.0)
    spread = jnp.where(jnp.logical_and(from_d, jnp.logical_not(inner)), 0.0, spread)
    sh, sl = halves(spread)
    spread3 = jnp.concatenate([sh, sh, sl], axis=0)
    mh, ml = halves(jnp.concatenate([got_c[...], got_d[...]], axis=0))
    sums3 = jnp.concatenate([mh, ml, mh], axis=0)

    i = lax.broadcasted_iota(jnp.int32, (rows, lanes), 0)
    fall_l, fall_r = power(i), power(rows - 1 - i)
    hit_l, hit_r = jnp.where(i == 0, 1.0, 0.0), jnp.where(i == rows - 1, 1.0, 0.0)
    ta, ea = jnp.where(even_x, fall_r, fall_l), jnp.where(even_x, hit_r, hit_l)
    tb, eb = jnp.where(even_x, fall_l, fall_r), jnp.where(even_x, hit_l, hit_r)

    def xc(f, k):
        at = lambda ref, kind: ref[pl.ds((2 * f + kind) * depth + k, 1), :]
        return ta * at(got_a, 0) + ea * at(got_a, 1) + tb * at(got_b, 0) + eb * at(got_b, 1)

    group = 2
    tn = (((0,), (0,)), ((), ()))
    for g in range(depth // group):
        span = group * rows
        yc = lax.dot_general(
            sums3[:, g * span : (g + 1) * span], spread3, tn, preferred_element_type=f32
        )
        for q in range(group):
            k = g * group + q
            part = lambda t: yc[q * rows : (q + 1) * rows, t * lanes : (t + 1) * lanes]
            lz_s[k] = lz[k] + part(0) - by * xc(3, k)
            vx_s[k] = vx[k] + part(1)
            vy_s[k] = vy[k] - xc(2, k)
            vz_s[k] = vz[k] + part(2) + xc(1, k)
            dv_s[k] = dv[k] + part(3) + xc(0, k)
    copies = [
        pltpu.make_async_copy(s, d, sems.at[n])
        for n, (s, d) in enumerate(
            [
                (lz_s, lorentz.at[2]),
                (vx_s, vorticity.at[0]),
                (vy_s, vorticity.at[1]),
                (vz_s, vorticity.at[2]),
                (dv_s, divergence),
            ]
        )
    ]
    for c in copies:
        c.start()
    for c in copies:
        c.wait()


def local(wx, wy, ring, line, u, v, w, p):
    depth, rows, lanes = u.shape
    block = (depth, rows, lanes)
    vmem = pl.BlockSpec(memory_space=pltpu.VMEM)
    anywhere = pl.BlockSpec(memory_space=pl.ANY)
    params = pltpu.CompilerParams(vmem_limit_bytes=24 * 2**20)
    keep = lambda x: pltpu.with_memory_space_constraint(x, pltpu.VMEM)
    size = 4 * depth * rows * lanes

    fields, msg_a, msg_b, msg_c, msg_d = pl.pallas_call(
        edges_kernel,
        name="edge_sums",
        out_shape=(
            pltpu.VMEM((4,) + block, f32),
            pltpu.VMEM((8 * depth, lanes), f32),
            pltpu.VMEM((8 * depth, lanes), f32),
            pltpu.VMEM((8, depth * rows), f32),
            pltpu.VMEM((8, depth * rows), f32),
        ),
        in_specs=[anywhere] * 4,
        out_specs=(vmem,) * 5,
        scratch_shapes=[pltpu.SemaphoreType.DMA((4,))],
        compiler_params=params,
        cost_estimate=pl.CostEstimate(flops=8 * size, bytes_accessed=4 * size, transcendentals=0),
    )(u, v, w, p)

    pairs_a = [(i, i ^ 1) for i in range(ring)]
    pairs_b = [(i, (i + 1) % ring if i % 2 else (i - 1) % ring) for i in range(ring)]
    pairs_c = [(i, i ^ 1) for i in range(line)]
    pairs_d = [(i, (i + 1) % line if i % 2 else (i - 1) % line) for i in range(line)]
    got_b = lax.ppermute(msg_b, "gx", pairs_b)
    got_a = lax.ppermute(msg_a, "gx", pairs_a)
    got_c = lax.ppermute(msg_c, "gy", pairs_c)
    got_d = lax.ppermute(msg_d, "gy", pairs_d)

    lorentz, lz, vx, vy, vz, dv = pl.pallas_call(
        local_kernel,
        name="own_block",
        out_shape=(jax.ShapeDtypeStruct((3,) + block, f32),) + (pltpu.VMEM(block, f32),) * 5,
        in_specs=[vmem, vmem, anywhere],
        out_specs=(anywhere,) + (vmem,) * 5,
        scratch_shapes=[
            pltpu.VMEM((2 * lanes, 2 * lanes), bf16),
            pltpu.VMEM(block, f32),
            pltpu.VMEM(block, f32),
            pltpu.SemaphoreType.DMA((3,)),
        ],
        compiler_params=params,
        cost_estimate=pl.CostEstimate(flops=800 * size, bytes_accessed=12 * size, transcendentals=0),
    )(keep(fields), jnp.asarray(wx), jnp.asarray(wy))

    return pl.pallas_call(
        join_kernel,
        name="join",
        out_shape=(
            jax.ShapeDtypeStruct((3,) + block, f32),
            jax.ShapeDtypeStruct((3,) + block, f32),
            jax.ShapeDtypeStruct(block, f32),
        ),
        in_specs=[vmem] * 9 + [anywhere],
        out_specs=(anywhere,) * 3,
        scratch_shapes=[pltpu.VMEM(block, f32)] * 5 + [pltpu.SemaphoreType.DMA((5,))],
        input_output_aliases={9: 0},
        compiler_params=params,
        cost_estimate=pl.CostEstimate(flops=30 * size, bytes_accessed=12 * size, transcendentals=0),
    )(
        *(keep(x) for x in (got_a, got_b, got_c, got_d, lz, vx, vy, vz, dv)),
        lorentz,
    )


def solution(mesh):
    ring, line = mesh.shape["gx"], mesh.shape["gy"]
    cells = P(None, "gx", "gy")
    stacked = P(None, None, "gx", "gy")
    wx = x_operator(4096 // ring)
    wy = y_operators(512, line)
    return jax.shard_map(
        functools.partial(local, wx, wy, ring, line),
        mesh=mesh,
        in_specs=(cells,) * 4,
        out_specs=(stacked, stacked, cells),
        check_vma=False,
    )
```

time: 1340 us -> 23.2 us (0.02)
  the two profiles are of different devices: /device:TPU:1 before, /device:TPU:6 now
where the time goes in v1:
time: 23.2 us; the launch traced here: 22.9 us
  starting transfers between devices  10.5 us (45%)
  Pallas kernels  5.33 us (23%)
  local copies, waits for them, and re-layouts  4.17 us (18%)
  waiting for transfers between devices  2.25 us (10%)
  between operations  0.67 us (3%)
    ppermute x1, starting transfers between devices, local(): got_b = lax.ppermute(msg_b, 'gx', pairs_b)  8.41 us
    unnamed x12, local copies, waits for them, and re-layouts  4.17 us
    pallas_call x1, Pallas kernels, local(): pl.pallas_call(join_kernel, name='join', out_shape=(jax.ShapeDtypeStruct(...  2.15 us
    ppermute x1, waiting for transfers between devices, local(): got_d = lax.ppermute(msg_d, 'gy', pairs_d)  2.04 us
    pallas_call x1, Pallas kernels, local(): pl.pallas_call(local_kernel, name='own_block', out_shape=(jax.ShapeDtypeS...  1.73 us
    pallas_call x1, Pallas kernels, local(): pl.pallas_call(edges_kernel, name='edge_sums', out_shape=(pltpu.VMEM((4,)...  1.45 us
    ppermute x1, starting transfers between devices, local(): got_d = lax.ppermute(msg_d, 'gy', pairs_d)  1.14 us
    ppermute x1, starting transfers between devices, local(): got_c = lax.ppermute(msg_c, 'gy', pairs_c)  0.83 us
  transfers between devices with their start and end apart: 4, of which 2 were waited for; matrix products, arithmetic and copies ran while one was open for 0% of the time, Pallas kernels for 8%

profile of v1, /device:TPU:6, one launch (start us, length us, event | category | flops | bytes accessed | tf_op | source)
XLA Modules:
  0.0 22.9 jit_solution(6011869433654814094)
XLA Ops:
  0.6 0.0 copy-start
  0.6 1.0 %copy-done = f32[16,64,128]{2,1,0:T(8,128)S(1)} copy-done((f32[16,64,128]{2,1,0:T(8,128)S(1)}, f32[16,64,128]{2,1,0:T(8,128)}, u32[]{:S(2)}) %copy-start) | copy-done | bytes 524312
  1.7 0.0 copy-start.1
  1.7 1.0 %copy-done.1 = f32[16,64,128]{2,1,0:T(8,128)S(1)} copy-done((f32[16,64,128]{2,1,0:T(8,128)S(1)}, f32[16,64,128]{2,1,0:T(8,128)}, u32[]{:S(2)}) %copy-start.1) | copy-done | bytes 524312
  2.7 0.0 copy-start.2
  2.7 1.0 %copy-done.2 = f32[16,64,128]{2,1,0:T(8,128)S(1)} copy-done((f32[16,64,128]{2,1,0:T(8,128)S(1)}, f32[16,64,128]{2,1,0:T(8,128)}, u32[]{:S(2)}) %copy-start.2) | copy-done | bytes 524312
  3.8 0.0 copy-start.3
  3.8 1.0 %copy-done.3 = f32[16,64,128]{2,1,0:T(8,128)S(1)} copy-done((f32[16,64,128]{2,1,0:T(8,128)S(1)}, f32[16,64,128]{2,1,0:T(8,128)}, u32[]{:S(2)}) %copy-start.3) | copy-done | bytes 524312
  4.8 0.0 copy-start.4
  4.8 0.0 copy-start.5
  4.8 1.4 %edge_sums.1 = (f32[4,16,64,128]{3,2,1,0:T(8,128)S(1)}, f32[128,128]{1,0:T(8,128)S(1)}, f32[128,128]{1,0:T(8,128)S(1)}, f32[8,1024]{1,0:T(8,128)S(1)}, f32[8,1024]{1,0:T(8,128)S(1)}) custom-call(f32[16,64,128]{2,1,0:T(8,128)S(1)} %copy-done, f32[16,64,128]{2,1,0:T(8,128)S(1)} %copy-done.1, f32[16,64,128]{2,1,0:T(8,128)S(1)} %copy-done.2, ...), custom_call_target="tpu_custom_call" | custom-call | flops 4194304 | bytes 2097152 | tf_op jit(solution)/shard_map/edge_sums/pallas_call | solution.py:246
  6.3 0.1 collective-permute-start
  6.4 8.4 %collective-permute-start.1 = (f32[128,128]{1,0:T(8,128)S(1)}, f32[128,128]{1,0:T(8,128)S(1)}, u32[]{:S(2)}, u32[]{:S(2)}) collective-permute-start(f32[128,128]{1,0:T(8,128)S(1)} %get-tuple-element.15), channel_id=1, source_target_pairs={{0,252},{4,8},{8,4},{12,16},{16,12},{20,24},{24,20},{28,32},{32,28... | collective-permute-start | bytes 196616 | tf_op jit(solution)/shard_map/ppermute | solution.py:267
  14.8 0.8 %collective-permute-start.2 = (f32[8,1024]{1,0:T(8,128)S(1)}, f32[8,1024]{1,0:T(8,128)S(1)}, u32[]{:S(2)}, u32[]{:S(2)}) collective-permute-start(f32[8,1024]{1,0:T(8,128)S(1)} %get-tuple-element.16), channel_id=1, source_target_pairs={{0,1},{1,0},{2,3},{3,2},{4,5},{5,4},{6,7},{7,6},{8,9},{9,8},{10,11... | collective-permute-start | bytes 98312 | tf_op jit(solution)/shard_map/ppermute | solution.py:269
  15.6 1.1 %collective-permute-start.3 = (f32[8,1024]{1,0:T(8,128)S(1)}, f32[8,1024]{1,0:T(8,128)S(1)}, u32[]{:S(2)}, u32[]{:S(2)}) collective-permute-start(f32[8,1024]{1,0:T(8,128)S(1)} %get-tuple-element.17), channel_id=1, source_target_pairs={{0,3},{1,2},{2,1},{3,0},{4,7},{5,6},{6,5},{7,4},{8,11},{9,10},{10,... | collective-permute-start | bytes 98312 | tf_op jit(solution)/shard_map/ppermute | solution.py:270
  16.7 0.0 copy-done.4
  16.7 0.0 copy-done.5
  16.7 1.7 %own_block.1 = (f32[3,16,64,128]{3,2,1,0:T(8,128)}, f32[16,64,128]{2,1,0:T(8,128)S(1)}, f32[16,64,128]{2,1,0:T(8,128)S(1)}, f32[16,64,128]{2,1,0:T(8,128)S(1)}, ...) custom-call(f32[4,16,64,128]{3,2,1,0:T(8,128)S(1)} %get-tuple-element.18.fields, bf16[64,192]{1,0:T(8,128)(2,1)S(1)} %copy-done.5, ...), custom_call_target="tpu_custom_call" | custom-call | flops 419430400 | bytes 6291456 | tf_op jit(solution)/shard_map/own_block/pallas_call | solution.py:272
  18.5 0.2 collective-permute-done.2.got_c
  18.7 2.0 %collective-permute-done.3.got_d = f32[8,1024]{1,0:T(8,128)S(1)} collective-permute-done((f32[8,1024]{1,0:T(8,128)S(1)}, f32[8,1024]{1,0:T(8,128)S(1)}, u32[]{:S(2)}, u32[]{:S(2)}) %collective-permute-start.3) | collective-permute-done | bytes 32800 | tf_op jit(solution)/shard_map/ppermute | solution.py:270
  20.7 0.0 collective-permute-done.got_a
  20.7 0.0 collective-permute-done.1.got_b
  20.7 2.2 %join.1 = (f32[3,16,64,128]{3,2,1,0:T(8,128)}, f32[3,16,64,128]{3,2,1,0:T(8,128)}, f32[16,64,128]{2,1,0:T(8,128)}) custom-call(f32[128,128]{1,0:T(8,128)S(1)} %collective-permute-done.got_a, f32[128,128]{1,0:T(8,128)S(1)} %collective-permute-done.1.got_b, f32[8,1024]{1,0:T(8,128)S(1)} %collective-permute-done.2.got_c, ...), custom_call_target="tpu_custom_call", output_to_operand_aliasing={{0}: (9, {})} | custom-call | flops 15728640 | bytes 6291456 | tf_op jit(solution)/shard_map/join/pallas_call | solution.py:288
Async XLA Ops:
  0.6 1.0 %copy-start = (f32[16,64,128]{2,1,0:T(8,128)S(1)}, f32[16,64,128]{2,1,0:T(8,128)}, u32[]{:S(2)}) copy-start(f32[16,64,128]{2,1,0:T(8,128)} %u.1) | copy-start | bytes 1572868
  1.7 1.0 %copy-start.1 = (f32[16,64,128]{2,1,0:T(8,128)S(1)}, f32[16,64,128]{2,1,0:T(8,128)}, u32[]{:S(2)}) copy-start(f32[16,64,128]{2,1,0:T(8,128)} %v.1) | copy-start | bytes 1572868
  2.7 1.0 %copy-start.2 = (f32[16,64,128]{2,1,0:T(8,128)S(1)}, f32[16,64,128]{2,1,0:T(8,128)}, u32[]{:S(2)}) copy-start(f32[16,64,128]{2,1,0:T(8,128)} %w.1) | copy-start | bytes 1572868
  3.8 1.0 %copy-start.3 = (f32[16,64,128]{2,1,0:T(8,128)S(1)}, f32[16,64,128]{2,1,0:T(8,128)}, u32[]{:S(2)}) copy-start(f32[16,64,128]{2,1,0:T(8,128)} %p.1) | copy-start | bytes 1572868
  4.8 11.9 %copy-start.4 = (bf16[4,256,256]{2,1,0:T(8,128)(2,1)S(1)}, bf16[4,256,256]{2,1,0:T(8,128)(2,1)}, u32[]{:S(2)}) copy-start(bf16[4,256,256]{2,1,0:T(8,128)(2,1)} %constant.5.clone.wy_all) | copy-start | bytes 1572868
  4.8 11.9 %copy-start.5 = (bf16[64,192]{1,0:T(8,128)(2,1)S(1)}, bf16[64,192]{1,0:T(8,128)(2,1)}, u32[]{:S(2)}) copy-start(bf16[64,192]{1,0:T(8,128)(2,1)} %constant.4.clone.wx) | copy-start | bytes 73732
  6.3 14.5 %collective-permute-start = (f32[128,128]{1,0:T(8,128)S(1)}, f32[128,128]{1,0:T(8,128)S(1)}, u32[]{:S(2)}, u32[]{:S(2)}) collective-permute-start(f32[128,128]{1,0:T(8,128)S(1)} %get-tuple-element.14), channel_id=1, source_target_pairs={{0,4},{4,0},{8,12},{12,8},{16,20},{20,16},{24,28},{28,24},{32,36},... | collective-permute-start | bytes 196616 | tf_op jit(solution)/shard_map/ppermute | solution.py:268
  6.4 14.4 %collective-permute-start.1 = (f32[128,128]{1,0:T(8,128)S(1)}, f32[128,128]{1,0:T(8,128)S(1)}, u32[]{:S(2)}, u32[]{:S(2)}) collective-permute-start(f32[128,128]{1,0:T(8,128)S(1)} %get-tuple-element.15), channel_id=1, source_target_pairs={{0,252},{4,8},{8,4},{12,16},{16,12},{20,24},{24,20},{28,32},{32,28... | collective-permute-start | bytes 196616 | tf_op jit(solution)/shard_map/ppermute | solution.py:267
  14.8 3.9 %collective-permute-start.2 = (f32[8,1024]{1,0:T(8,128)S(1)}, f32[8,1024]{1,0:T(8,128)S(1)}, u32[]{:S(2)}, u32[]{:S(2)}) collective-permute-start(f32[8,1024]{1,0:T(8,128)S(1)} %get-tuple-element.16), channel_id=1, source_target_pairs={{0,1},{1,0},{2,3},{3,2},{4,5},{5,4},{6,7},{7,6},{8,9},{9,8},{10,11... | collective-permute-start | bytes 98312 | tf_op jit(solution)/shard_map/ppermute | solution.py:269
  15.6 5.1 %collective-permute-start.3 = (f32[8,1024]{1,0:T(8,128)S(1)}, f32[8,1024]{1,0:T(8,128)S(1)}, u32[]{:S(2)}, u32[]{:S(2)}) collective-permute-start(f32[8,1024]{1,0:T(8,128)S(1)} %get-tuple-element.17), channel_id=1, source_target_pairs={{0,3},{1,2},{2,1},{3,0},{4,7},{5,6},{6,5},{7,4},{8,11},{9,10},{10,... | collective-permute-start | bytes 98312 | tf_op jit(solution)/shard_map/ppermute | solution.py:270

commit v2 on v1

v2 whole, which is shorter than its diff:
```python
import functools
import math

import jax
import jax.numpy as jnp
import ml_dtypes
import numpy as np
from jax import lax
from jax.experimental import pallas as pl
from jax.experimental.pallas import tpu as pltpu
from jax.sharding import PartitionSpec as P

third = 1.0 / 3.0
near = 7.0 / 9.0
far = 1.0 / 36.0
bx = 0.6
by = 0.8

lam = (-3.0 + math.sqrt(5.0)) / 2.0
scale = 1.0 / (1.0 + 2.0 * third * lam)
log_lam = math.log(-lam)
gamma = scale * (near * (lam - 1.0 / lam) + far * (lam**2 - lam**-2))
edge = scale * (near * (lam**2 - 1.0) + far * (lam**3 - lam)) - gamma * lam

f32 = jnp.float32
bf16 = jnp.bfloat16
pieces = 2


def halves(values):
    high = values.astype(bf16)
    return high, (values - high.astype(f32)).astype(bf16)


def host_halves(values):
    values = values.astype(np.float32)
    high = values.astype(ml_dtypes.bfloat16)
    low = (values - high.astype(np.float32)).astype(ml_dtypes.bfloat16)
    return high, low


def x_operator(count):
    h = lambda m: scale * lam ** np.abs(m)
    i = np.arange(count)
    m = i[:, None] - i[None, :]
    own = near * (h(m + 1) - h(m - 1)) + far * (h(m + 2) - h(m - 2))
    high, low = host_halves(own)
    return np.concatenate([high, low, high], axis=1)


def y_operators(total, blocks):
    a = np.eye(total)
    b = np.zeros((total, total))
    for j in range(2, total - 2):
        a[j, j - 1] = a[j, j + 1] = third
        b[j, j + 1], b[j, j - 1], b[j, j + 2], b[j, j - 2] = near, -near, far, -far
    a[0, 1] = a[-1, -2] = 2.0
    b[0, :3] = -2.5, 2.0, 0.5
    b[-1, -3:] = -0.5, -2.0, 2.5
    for j in (1, total - 2):
        a[j, j - 1] = a[j, j + 1] = 0.25
        b[j, j + 1], b[j, j - 1] = 0.75, -0.75
    whole = np.linalg.solve(a, b)
    size = total // blocks
    out = []
    for g in range(blocks):
        own = whole[g * size : (g + 1) * size, g * size : (g + 1) * size].T
        high, low = host_halves(own)
        out.append(np.block([[high, low], [high, np.zeros_like(low)]]))
    return np.stack(out)


def power(n):
    size = jnp.exp(n.astype(f32) * log_lam)
    return jnp.where((n & 1) == 0, size, -size)


def x_message(f, msg, planes, at_right):
    depth, rows, lanes = f.shape
    k = lax.broadcasted_iota(jnp.int32, (rows, lanes), 0)
    weights = jnp.where(at_right, gamma * power(rows - k), -gamma * power(k + 1))
    msg[0, planes] = jnp.sum(f * weights[None], axis=1)
    msg[1, planes] = jnp.where(at_right, edge * f[:, rows - 1, :], -edge * f[:, 0, :])


def y_messages(fields, msg_c, msg_d):
    _, depth, rows, lanes = fields.shape
    even_y = lax.rem(lax.axis_index("gy"), 2) == 0
    j = lax.broadcasted_iota(jnp.int32, (8, lanes), 1)
    row = lax.broadcasted_iota(jnp.int32, (8, lanes), 0)
    odd = (row & 1) == 1
    y_right = jnp.where(odd, jnp.where(j == lanes - 1, edge, 0.0), gamma * power(lanes - j))
    y_left = jnp.where(odd, jnp.where(j == 0, -edge, 0.0), -gamma * power(j + 1))
    high, low = halves(jnp.where((row < 2) == even_y, y_right, y_left))
    both = jnp.concatenate([high, low], axis=0)
    nt = (((1,), (1,)), ((), ()))
    for i in range(4):
        fh, fl = halves(fields[i].reshape(depth * rows, lanes))
        top = lax.dot_general(both, fh, nt, preferred_element_type=f32)
        rest = lax.dot_general(both, fl, nt, preferred_element_type=f32)
        sums = top[0:8] + top[8:16] + rest[0:8]
        for b in range(depth * rows // lanes):
            part = sums[:, b * lanes : (b + 1) * lanes]
            msg_c[pl.ds(8 * b + 2 * i, 2), :] = part[0:2]
            msg_d[pl.ds(8 * b + 2 * i, 2), :] = part[2:4]


def edges_kernel(u, v, w, p, fields, chip, far_side, early_c, early_d, sems):
    depth, rows, lanes = u.shape
    piece = depth // pieces
    copies = [
        [
            pltpu.make_async_copy(
                s.at[pl.ds(n * piece, piece)],
                fields.at[i, pl.ds(n * piece, piece)],
                sems.at[i * pieces + n],
            )
            for n in range(pieces)
        ]
        for i, s in enumerate((u, v, w, p))
    ]
    for field in copies:
        for c in field:
            c.start()
    gx = lax.axis_index("gx")
    even_x = lax.rem(gx, 2) == 0
    early_d[...] = jnp.zeros_like(early_d)
    for i in range(4):
        for n in range(pieces):
            copies[i][n].wait()
            f = fields[i, pl.ds(n * piece, piece)]
            planes = pl.ds(n * piece, piece)
            x_message(f, chip.at[i], planes, even_x)
            x_message(f, far_side.at[i], planes, jnp.logical_not(even_x))

    @pl.when(gx < 2)
    def _():
        early_c[...] = jnp.zeros_like(early_c)
        y_messages(fields, early_c, early_d)

    @pl.when(gx >= 2)
    def _():
        early_c[...] = chip[...].reshape(early_c.shape)


def late_kernel(fields, chip, early_c, early_d, late_c, late_d):
    @pl.when(lax.axis_index("gx") < 2)
    def _():
        late_c[...] = chip[...].reshape(late_c.shape)
        late_d[...] = jnp.zeros_like(late_d)

    @pl.when(lax.axis_index("gx") >= 2)
    def _():
        y_messages(fields, late_c, late_d)


def own_kernel(fields, wx, wy_all, lorentz, lz_o, vx_o, vy_o, vz_o, dv_o, lx_s, ly_s, sems):
    _, depth, rows, lanes = fields.shape
    u, v, w, p = range(4)
    wy = wy_all.at[lax.axis_index("gy")]

    def dz(i, k):
        at = lambda s: fields[i, (k + s) % depth]
        return (
            0.75 * (at(1) - at(-1)) - 0.15 * (at(2) - at(-2)) + (1.0 / 60.0) * (at(3) - at(-3))
        )

    for k in range(depth):
        jz = by * fields[u, k] - bx * fields[v, k] - dz(p, k)
        lx_s[k] = -by * jz
        ly_s[k] = bx * jz
    put_x = pltpu.make_async_copy(lx_s, lorentz.at[0], sems.at[0])
    put_y = pltpu.make_async_copy(ly_s, lorentz.at[1], sems.at[1])
    put_x.start()
    put_y.start()
    for k in range(depth):
        split = [halves(fields[i, k]) for i in range(4)]
        highs = jnp.concatenate([s[0] for s in split], axis=0)
        lows = jnp.concatenate([s[1] for s in split], axis=0)
        y = jnp.dot(jnp.concatenate([highs, lows], axis=1), wy[...], preferred_element_type=f32)
        y = y[:, :lanes] + y[:, lanes:]
        wide_h = jnp.concatenate([s[0] for s in split], axis=1)
        wide_l = jnp.concatenate([s[1] for s in split], axis=1)
        x = jnp.dot(
            wx[...], jnp.concatenate([wide_h, wide_h, wide_l], axis=0), preferred_element_type=f32
        )
        yd = lambda i: y[i * rows : (i + 1) * rows]
        xd = lambda i: x[:, i * lanes : (i + 1) * lanes]
        lz_o[k] = bx * yd(p) - by * xd(p) - fields[w, k]
        vx_o[k] = yd(w) - dz(v, k)
        vy_o[k] = dz(u, k) - xd(w)
        vz_o[k] = xd(v) - yd(u)
        dv_o[k] = xd(u) + yd(v) + dz(w, k)
    put_x.wait()
    put_y.wait()


def hold_kernel(message, held):
    pass


def y_spread(lanes, line):
    out = []
    j = np.arange(lanes)
    for g in range(line):
        table = np.zeros((16, 4, lanes))
        for side in range(2):
            from_left = (side == 1) == (g % 2 == 0)
            if (from_left and g == 0) or (not from_left and g == line - 1):
                continue
            away = j if from_left else lanes - 1 - j
            for field, (target, factor) in enumerate(((2, -1.0), (3, 1.0), (1, 1.0), (0, bx))):
                table[8 * side + 2 * field, target] = factor * lam**away
                table[8 * side + 2 * field + 1, target] = factor * (away == 0)
        table = table.reshape(16, 4 * lanes)
        table[np.abs(table) < 1e-37] = 0.0
        high, low = host_halves(table)
        out.append(np.concatenate([high, high, low], axis=0))
    return np.stack(out)


def join_kernel(
    got_far, early_c, early_d, late_c, late_d, spread_all, lz, vx, vy, vz, dv, lorentz_in,
    lorentz, vorticity, divergence, lz_s, vx_s, vy_s, vz_s, dv_s, chip_s, sems
):
    depth, rows, lanes = lz.shape
    gx = lax.axis_index("gx")
    even_x = lax.rem(gx, 2) == 0
    first = gx < 2
    spread = spread_all[lax.axis_index("gy")]
    got_c = jnp.where(first, early_c[...], late_c[...])
    got_d = jnp.where(first, early_d[...], late_d[...])
    chip_s[...] = jnp.where(first, late_c[...], early_c[...])
    i = lax.broadcasted_iota(jnp.int32, (rows, lanes), 0)
    fall_l, fall_r = power(i), power(rows - 1 - i)
    fall_chip = jnp.where(even_x, fall_r, fall_l)
    fall_far = jnp.where(even_x, fall_l, fall_r)
    sub = lax.broadcasted_iota(jnp.int32, (8, lanes), 0)
    low_far = jnp.where(jnp.logical_and(sub == 0, even_x), 1.0, 0.0)
    low_chip = jnp.where(jnp.logical_and(sub == 0, jnp.logical_not(even_x)), 1.0, 0.0)
    high_far = jnp.where(jnp.logical_and(sub == 7, jnp.logical_not(even_x)), 1.0, 0.0)
    high_chip = jnp.where(jnp.logical_and(sub == 7, even_x), 1.0, 0.0)

    def xc(f, k):
        at = lambda ref, kind: ref[pl.ds((2 * f + kind) * depth + k, 1), :]
        c = fall_far * at(got_far, 0) + fall_chip * at(chip_s, 0)
        far_e, chip_e = at(got_far, 1), at(chip_s, 1)
        head = c[:8] + low_far * far_e + low_chip * chip_e
        tail = c[rows - 8 :] + high_far * far_e + high_chip * chip_e
        return jnp.concatenate([head, c[8 : rows - 8], tail], axis=0)

    group = 4
    per = lanes // rows
    tn = (((0,), (0,)), ((), ()))
    copies = []
    for g in range(depth // group):
        for k in range(g * group, (g + 1) * group):
            b, q = k // per, k % per
            if q == 0:
                got = [m[8 * b : 8 * b + 8] for m in (got_c, got_d)]
                high, low = halves(jnp.concatenate(got, axis=0))
                sums = jnp.concatenate([high, low, high], axis=0)
                yc = lax.dot_general(sums, spread, tn, preferred_element_type=f32)
            part = lambda t: yc[q * rows : (q + 1) * rows, t * lanes : (t + 1) * lanes]
            lz_s[k] = lz[k] + part(0) - by * xc(3, k)
            vx_s[k] = vx[k] + part(1)
            vy_s[k] = vy[k] - xc(2, k)
            vz_s[k] = vz[k] + part(2) + xc(1, k)
            dv_s[k] = dv[k] + part(3) + xc(0, k)
        planes = pl.ds(g * group, group)
        for s, d in (
            (lz_s, lorentz.at[2]),
            (vx_s, vorticity.at[0]),
            (vy_s, vorticity.at[1]),
            (vz_s, vorticity.at[2]),
            (dv_s, divergence),
        ):
            c = pltpu.make_async_copy(s.at[planes], d.at[planes], sems.at[len(copies)])
            c.start()
            copies.append(c)
    for c in copies:
        c.wait()


def local(wx, wy, spread, ring, line, u, v, w, p):
    depth, rows, lanes = u.shape
    block = (depth, rows, lanes)
    vmem = pl.BlockSpec(memory_space=pltpu.VMEM)
    anywhere = pl.BlockSpec(memory_space=pl.ANY)
    params = pltpu.CompilerParams(vmem_limit_bytes=24 * 2**20)
    keep = lambda x: pltpu.with_memory_space_constraint(x, pltpu.VMEM)
    stay = lambda x: pltpu.with_memory_space_constraint(x, pltpu.HBM)
    size = 4 * depth * rows * lanes
    cost = lambda flops, moved: pl.CostEstimate(
        flops=flops * size, bytes_accessed=moved * size, transcendentals=0
    )
    wx, wy, spread = (keep(jnp.asarray(t)) for t in (wx, wy, spread))
    msg = pltpu.VMEM((8 * depth, lanes), f32)
    x_msg = pltpu.VMEM((4, 2, depth, lanes), f32)
    half = pltpu.VMEM((4 * depth, lanes), f32)

    def over_chips(column):
        return [
            (i * line + j, column(i, j)[0] * line + column(i, j)[1])
            for i in range(ring)
            for j in range(line)
        ]

    mate = lambda i, j: (i ^ 1, j)
    y_one = lambda i, j: (i, j ^ 1)
    y_two = lambda i, j: (i, (j + 1) % line if j % 2 else (j - 1) % line)
    first = lambda a, b: over_chips(lambda i, j: a(i, j) if i < 2 else b(i, j))
    both = ("gx", "gy")

    fields, chip, far_side, early_c, early_d = pl.pallas_call(
        edges_kernel,
        name="edge_sums",
        out_shape=(pltpu.VMEM((4,) + block, f32), x_msg, x_msg, msg, half),
        in_specs=[anywhere] * 4,
        out_specs=(vmem,) * 5,
        scratch_shapes=[pltpu.SemaphoreType.DMA((4 * pieces,))],
        compiler_params=params,
        cost_estimate=cost(1, 1),
    )(*(stay(x) for x in (u, v, w, p)))
    early_c = lax.ppermute(early_c, both, first(y_one, mate))
    early_d = lax.ppermute(early_d, both, first(y_two, mate))

    far_side = pl.pallas_call(
        hold_kernel,
        name="hold",
        out_shape=x_msg,
        in_specs=[vmem],
        out_specs=vmem,
        input_output_aliases={0: 0},
        compiler_params=params,
        cost_estimate=cost(1, 1),
    )(keep(far_side))
    got_far = lax.ppermute(
        far_side, "gx", [(i, (i + 1) % ring if i % 2 else (i - 1) % ring) for i in range(ring)]
    )

    late_c, late_d = pl.pallas_call(
        late_kernel,
        name="y_sums",
        out_shape=(msg, half),
        in_specs=[vmem, vmem, anywhere, anywhere],
        out_specs=(vmem,) * 2,
        compiler_params=params,
        cost_estimate=cost(1, 1),
    )(*(keep(x) for x in (fields, chip, early_c, early_d)))
    late_c = lax.ppermute(late_c, both, first(mate, y_one))
    late_d = lax.ppermute(late_d, both, first(mate, y_two))

    lorentz, *part = pl.pallas_call(
        own_kernel,
        name="own_block",
        out_shape=(jax.ShapeDtypeStruct((3,) + block, f32),) + (pltpu.VMEM(block, f32),) * 5,
        in_specs=[vmem] * 3,
        out_specs=(anywhere,) + (vmem,) * 5,
        scratch_shapes=[
            pltpu.VMEM(block, f32),
            pltpu.VMEM(block, f32),
            pltpu.SemaphoreType.DMA((2,)),
        ],
        compiler_params=params,
        cost_estimate=cost(4000, 12),
    )(keep(fields), wx, wy)

    got_far = got_far.reshape(msg.shape)
    return pl.pallas_call(
        join_kernel,
        name="join",
        out_shape=(
            jax.ShapeDtypeStruct((3,) + block, f32),
            jax.ShapeDtypeStruct((3,) + block, f32),
            jax.ShapeDtypeStruct(block, f32),
        ),
        in_specs=[vmem] * 11 + [anywhere],
        out_specs=(anywhere,) * 3,
        scratch_shapes=[pltpu.VMEM(block, f32)] * 5
        + [pltpu.VMEM(msg.shape, f32), pltpu.SemaphoreType.DMA((20,))],
        input_output_aliases={11: 0},
        compiler_params=params,
        cost_estimate=cost(30, 12),
    )(
        *(keep(x) for x in (got_far, early_c, early_d, late_c, late_d)),
        spread,
        *(keep(x) for x in part),
        lorentz,
    )


def solution(mesh):
    ring, line = mesh.shape["gx"], mesh.shape["gy"]
    cells = P(None, "gx", "gy")
    stacked = P(None, None, "gx", "gy")
    wx = x_operator(4096 // ring)
    wy = y_operators(512, line)
    spread = y_spread(512 // line, line)
    return jax.shard_map(
        functools.partial(local, wx, wy, spread, ring, line),
        mesh=mesh,
        in_specs=(cells,) * 4,
        out_specs=(stacked, stacked, cells),
        check_vma=False,
    )
```

time: 23.2 us -> 17.3 us (0.75)
  the two profiles are of different devices: /device:TPU:6 before, /device:TPU:1 now
where the time goes in v2:
time: 17.3 us; the launch traced here: 17.2 us
  starting transfers between devices  7.5 us (43%)
  Pallas kernels  6.78 us (39%)
  waiting for transfers between devices  2.17 us (13%)
  between operations  0.71 us (4%)
    ppermute x1, starting transfers between devices, local(): late_d = lax.ppermute(late_d, both, first(mate, y_two))  3.44 us
    pallas_call x1, Pallas kernels, local(): pl.pallas_call(own_kernel, name='own_block', out_shape=(jax.ShapeDtypeStr...  2.52 us
    pallas_call x1, Pallas kernels, local(): pl.pallas_call(edges_kernel, name='edge_sums', out_shape=(pltpu.VMEM((4,)...  2.31 us
    ppermute x1, waiting for transfers between devices, local(): early_d = lax.ppermute(early_d, both, first(y_two, mate))  2.16 us
    ppermute x1, starting transfers between devices, local(): early_c = lax.ppermute(early_c, both, first(y_one, mate))  2.13 us
    pallas_call x1, Pallas kernels, local(): pl.pallas_call(join_kernel, name='join', out_shape=(jax.ShapeDtypeStruct(...  1.94 us
    ppermute x1, starting transfers between devices, local(): early_d = lax.ppermute(early_d, both, first(y_two, mate))  1.82 us
  transfers between devices with their start and end apart: 5, of which 1 were waited for; matrix products, arithmetic and copies ran while one was open for 0% of the time, Pallas kernels for 15%

profile of v2, /device:TPU:1, one launch (start us, length us, event | category | flops | bytes accessed | tf_op | source)
XLA Modules:
  0.0 17.2 jit_solution(10589885242060706023)
XLA Ops:
  0.6 2.3 %edge_sums.1 = (f32[4,16,64,128]{3,2,1,0:T(8,128)S(1)}, f32[4,2,16,128]{3,2,1,0:T(8,128)S(1)}, f32[4,2,16,128]{3,2,1,0:T(8,128)S(1)}, f32[128,128]{1,0:T(8,128)S(1)}, f32[64,128]{1,0:T(8,128)S(1)}) custom-call(f32[16,64,128]{2,1,0:T(8,128)} %u.1, f32[16,64,128]{2,1,0:T(8,128)} %v.1, f32[16,64,128]{2,1,0:T(8,128)} %w.1, f32[16,64,128]{2,1,0:T(8,128)} %p.1), custom_call_target="tpu_custom_call" | custom-call | flops 524288 | bytes 524288 | tf_op jit(solution)/shard_map/edge_sums/pallas_call | solution.py:315
  2.9 0.0 copy-start.1
  3.0 0.0 copy-start.2
  3.0 2.1 %collective-permute-start.1 = (f32[128,128]{1,0:T(8,128)S(1)}, f32[128,128]{1,0:T(8,128)S(1)}, u32[]{:S(2)}, u32[]{:S(2)}) collective-permute-start(f32[128,128]{1,0:T(8,128)S(1)} %get-tuple-element.17), channel_id=1, source_target_pairs={{0,1},{1,0},{2,3},{3,2},{4,5},{5,4},{6,7},{7,6},{8,12},{9,13},{10,... | collective-permute-start | bytes 196616 | tf_op jit(solution)/shard_map/ppermute | solution.py:325
  5.1 1.8 %collective-permute-start.2 = (f32[64,128]{1,0:T(8,128)S(1)}, f32[64,128]{1,0:T(8,128)S(1)}, u32[]{:S(2)}, u32[]{:S(2)}) collective-permute-start(f32[64,128]{1,0:T(8,128)S(1)} %get-tuple-element.18), channel_id=1, source_target_pairs={{0,3},{1,2},{2,1},{3,0},{4,7},{5,6},{6,5},{7,4},{8,12},{9,13},{10,... | collective-permute-start | bytes 98312 | tf_op jit(solution)/shard_map/ppermute | solution.py:326
  6.9 0.0 collective-permute-start
  6.9 2.2 %collective-permute-done.2.early_d = f32[64,128]{1,0:T(8,128)S(1)} collective-permute-done((f32[64,128]{1,0:T(8,128)S(1)}, f32[64,128]{1,0:T(8,128)S(1)}, u32[]{:S(2)}, u32[]{:S(2)}) %collective-permute-start.2) | collective-permute-done | bytes 32800 | tf_op jit(solution)/shard_map/ppermute | solution.py:326
  9.1 0.0 collective-permute-done.1.early_c
  9.1 3.4 %collective-permute-start.4 = (f32[64,128]{1,0:T(8,128)S(1)}, f32[64,128]{1,0:T(8,128)S(1)}, u32[]{:S(2)}, u32[]{:S(2)}) collective-permute-start(f32[64,128]{1,0:T(8,128)S(1)} %get-tuple-element.22), channel_id=1, source_target_pairs={{0,4},{1,5},{2,6},{3,7},{4,0},{5,1},{6,2},{7,3},{8,11},{9,10},{10,... | collective-permute-start | bytes 98312 | tf_op jit(solution)/shard_map/ppermute | solution.py:352
  12.5 0.0 copy-start
  12.5 0.1 collective-permute-start.3
  12.7 0.0 copy-done.1
  12.7 0.0 copy-done.2
  12.7 2.5 %own_block.1 = (f32[3,16,64,128]{3,2,1,0:T(8,128)}, f32[16,64,128]{2,1,0:T(8,128)S(1)}, f32[16,64,128]{2,1,0:T(8,128)S(1)}, f32[16,64,128]{2,1,0:T(8,128)S(1)}, ...) custom-call(f32[4,16,64,128]{3,2,1,0:T(8,128)S(1)} %get-tuple-element.19.fields, bf16[64,192]{1,0:T(8,128)(2,1)S(1)} %copy-done.2, ...), custom_call_target="tpu_custom_call" | custom-call | flops 2097152000 | bytes 6291456 | tf_op jit(solution)/shard_map/own_block/pallas_call | solution.py:354
  15.2 0.0 collective-permute-done
  15.2 0.0 collective-permute-done.4.late_d
  15.2 0.0 collective-permute-done.3.late_c
  15.2 0.0 copy-done
  15.2 1.9 %join.1 = (f32[3,16,64,128]{3,2,1,0:T(8,128)}, f32[3,16,64,128]{3,2,1,0:T(8,128)}, f32[16,64,128]{2,1,0:T(8,128)}) custom-call(f32[128,128]{1,0:T(8,128)S(1)} %bitcast.1, f32[128,128]{1,0:T(8,128)S(1)} %collective-permute-done.1.early_c, f32[64,128]{1,0:T(8,128)S(1)} %collective-permute-done.2.early_d, ...), custom_call_target="tpu_custom_call", output_to_operand_aliasing={{0}: (11, {})} | custom-call | flops 15728640 | bytes 6291456 | tf_op jit(solution)/shard_map/join/pallas_call | solution.py:370
  (2 shorter events, 0.0 us)
Async XLA Ops:
  2.9 9.7 %copy-start.1 = (bf16[4,256,256]{2,1,0:T(8,128)(2,1)S(1)}, bf16[4,256,256]{2,1,0:T(8,128)(2,1)}, u32[]{:S(2)}) copy-start(bf16[4,256,256]{2,1,0:T(8,128)(2,1)} %constant.7.clone.wy_all) | copy-start | bytes 1572868
  3.0 9.7 %copy-start.2 = (bf16[64,192]{1,0:T(8,128)(2,1)S(1)}, bf16[64,192]{1,0:T(8,128)(2,1)}, u32[]{:S(2)}) copy-start(bf16[64,192]{1,0:T(8,128)(2,1)} %constant.6.clone.wx) | copy-start | bytes 73732
  3.0 6.1 %collective-permute-start.1 = (f32[128,128]{1,0:T(8,128)S(1)}, f32[128,128]{1,0:T(8,128)S(1)}, u32[]{:S(2)}, u32[]{:S(2)}) collective-permute-start(f32[128,128]{1,0:T(8,128)S(1)} %get-tuple-element.17), channel_id=1, source_target_pairs={{0,1},{1,0},{2,3},{3,2},{4,5},{5,4},{6,7},{7,6},{8,12},{9,13},{10,... | collective-permute-start | bytes 196616 | tf_op jit(solution)/shard_map/ppermute | solution.py:325
  5.1 4.0 %collective-permute-start.2 = (f32[64,128]{1,0:T(8,128)S(1)}, f32[64,128]{1,0:T(8,128)S(1)}, u32[]{:S(2)}, u32[]{:S(2)}) collective-permute-start(f32[64,128]{1,0:T(8,128)S(1)} %get-tuple-element.18), channel_id=1, source_target_pairs={{0,3},{1,2},{2,1},{3,0},{4,7},{5,6},{6,5},{7,4},{8,12},{9,13},{10,... | collective-permute-start | bytes 98312 | tf_op jit(solution)/shard_map/ppermute | solution.py:326
  6.9 8.3 %collective-permute-start = (f32[4,2,16,128]{3,2,1,0:T(8,128)S(1)}, f32[4,2,16,128]{3,2,1,0:T(8,128)S(1)}, u32[]{:S(2)}, u32[]{:S(2)}) collective-permute-start(f32[4,2,16,128]{3,2,1,0:T(8,128)S(1)} %hold.1), channel_id=1, source_target_pairs={{0,252},{4,8},{8,4},{12,16},{16,12},{20,24},{24,20},{28,32},{32,28... | collective-permute-start | bytes 196616 | tf_op jit(solution)/shard_map/ppermute | solution.py:338
  9.1 6.1 %collective-permute-start.4 = (f32[64,128]{1,0:T(8,128)S(1)}, f32[64,128]{1,0:T(8,128)S(1)}, u32[]{:S(2)}, u32[]{:S(2)}) collective-permute-start(f32[64,128]{1,0:T(8,128)S(1)} %get-tuple-element.22), channel_id=1, source_target_pairs={{0,4},{1,5},{2,6},{3,7},{4,0},{5,1},{6,2},{7,3},{8,11},{9,10},{10,... | collective-permute-start | bytes 98312 | tf_op jit(solution)/shard_map/ppermute | solution.py:352
  12.5 2.7 %copy-start = (bf16[4,48,512]{2,1,0:T(8,128)(2,1)S(1)}, bf16[4,48,512]{2,1,0:T(8,128)(2,1)}, u32[]{:S(2)}) copy-start(bf16[4,48,512]{2,1,0:T(8,128)(2,1)} %constant.8.clone.spread_all) | copy-start | bytes 589828
  12.5 2.7 %collective-permute-start.3 = (f32[128,128]{1,0:T(8,128)S(1)}, f32[128,128]{1,0:T(8,128)S(1)}, u32[]{:S(2)}, u32[]{:S(2)}) collective-permute-start(f32[128,128]{1,0:T(8,128)S(1)} %get-tuple-element.21), channel_id=1, source_target_pairs={{0,4},{1,5},{2,6},{3,7},{4,0},{5,1},{6,2},{7,3},{8,9},{9,8},{10,11... | collective-permute-start | bytes 196616 | tf_op jit(solution)/shard_map/ppermute | solution.py:351

commit v3 on v2

--- a/solution.py
+++ b/solution.py
@@ -24,7 +24,9 @@
 
 f32 = jnp.float32
 bf16 = jnp.bfloat16
-pieces = 2
+pieces = 1
+own_step = 8
+join_groups = (2, 2, 2, 2, 2, 2, 2, 2)
 
 
 def halves(values):
@@ -160,20 +162,25 @@
     wy = wy_all.at[lax.axis_index("gy")]
 
     def dz(i, k):
-        at = lambda s: fields[i, (k + s) % depth]
+        at = lambda s: fields[i, (k + s) & (depth - 1)]
         return (
             0.75 * (at(1) - at(-1)) - 0.15 * (at(2) - at(-2)) + (1.0 / 60.0) * (at(3) - at(-3))
         )
 
-    for k in range(depth):
-        jz = by * fields[u, k] - bx * fields[v, k] - dz(p, k)
-        lx_s[k] = -by * jz
-        ly_s[k] = bx * jz
+
+    @pl.loop(0, depth, step=own_step)
+    def _(start):
+        for n in range(own_step):
+            k = start + n
+            jz = by * fields[u, k] - bx * fields[v, k] - dz(p, k)
+            lx_s[k] = -by * jz
+            ly_s[k] = bx * jz
+
     put_x = pltpu.make_async_copy(lx_s, lorentz.at[0], sems.at[0])
     put_y = pltpu.make_async_copy(ly_s, lorentz.at[1], sems.at[1])
     put_x.start()
     put_y.start()
-    for k in range(depth):
+    def plane(k):
         split = [halves(fields[i, k]) for i in range(4)]
         highs = jnp.concatenate([s[0] for s in split], axis=0)
         lows = jnp.concatenate([s[1] for s in split], axis=0)
@@ -191,6 +198,12 @@
         vy_o[k] = dz(u, k) - xd(w)
         vz_o[k] = xd(v) - yd(u)
         dv_o[k] = xd(u) + yd(v) + dz(w, k)
+
+    @pl.loop(0, depth, step=own_step)
+    def _(start):
+        for n in range(own_step):
+            plane(start + n)
+
     put_x.wait()
     put_y.wait()
 
@@ -221,15 +234,15 @@
 
 def join_kernel(
     got_far, early_c, early_d, late_c, late_d, spread_all, lz, vx, vy, vz, dv, lorentz_in,
-    lorentz, vorticity, divergence, lz_s, vx_s, vy_s, vz_s, dv_s, chip_s, sems
+    lorentz, vorticity, divergence, lz_s, vx_s, vy_s, vz_s, dv_s, chip_s, got_c, got_d, sems
 ):
     depth, rows, lanes = lz.shape
     gx = lax.axis_index("gx")
     even_x = lax.rem(gx, 2) == 0
     first = gx < 2
     spread = spread_all[lax.axis_index("gy")]
-    got_c = jnp.where(first, early_c[...], late_c[...])
-    got_d = jnp.where(first, early_d[...], late_d[...])
+    got_c[...] = jnp.where(first, early_c[: got_c.shape[0]], late_c[: got_c.shape[0]])
+    got_d[...] = jnp.where(first, early_d[...], late_d[...])
     chip_s[...] = jnp.where(first, late_c[...], early_c[...])
     i = lax.broadcasted_iota(jnp.int32, (rows, lanes), 0)
     fall_l, fall_r = power(i), power(rows - 1 - i)
@@ -249,15 +262,29 @@
         tail = c[rows - 8 :] + high_far * far_e + high_chip * chip_e
         return jnp.concatenate([head, c[8 : rows - 8], tail], axis=0)
 
-    group = 4
     per = lanes // rows
     tn = (((0,), (0,)), ((), ()))
-    copies = []
-    for g in range(depth // group):
-        for k in range(g * group, (g + 1) * group):
-            b, q = k // per, k % per
-            if q == 0:
-                got = [m[8 * b : 8 * b + 8] for m in (got_c, got_d)]
+    targets = (
+        (lz_s, lorentz.at[2]),
+        (vx_s, vorticity.at[0]),
+        (vy_s, vorticity.at[1]),
+        (vz_s, vorticity.at[2]),
+        (dv_s, divergence),
+    )
+
+    def puts(first_plane, last_plane):
+        planes = pl.ds(first_plane, last_plane - first_plane)
+        return [
+            pltpu.make_async_copy(s.at[planes], d.at[planes], sems.at[n])
+            for n, (s, d) in enumerate(targets)
+        ]
+
+    def group(first_plane, last_plane):
+        for k in range(first_plane, last_plane):
+            q = k % per
+            if q == 0 or k == first_plane:
+                rows_of = pl.ds(k // per * 8, 8)
+                got = [m[rows_of, :] for m in (got_c, got_d)]
                 high, low = halves(jnp.concatenate(got, axis=0))
                 sums = jnp.concatenate([high, low, high], axis=0)
                 yc = lax.dot_general(sums, spread, tn, preferred_element_type=f32)
@@ -267,18 +294,14 @@
             vy_s[k] = vy[k] - xc(2, k)
             vz_s[k] = vz[k] + part(2) + xc(1, k)
             dv_s[k] = dv[k] + part(3) + xc(0, k)
-        planes = pl.ds(g * group, group)
-        for s, d in (
-            (lz_s, lorentz.at[2]),
-            (vx_s, vorticity.at[0]),
-            (vy_s, vorticity.at[1]),
-            (vz_s, vorticity.at[2]),
-            (dv_s, divergence),
-        ):
-            c = pltpu.make_async_copy(s.at[planes], d.at[planes], sems.at[len(copies)])
+        for c in puts(first_plane, last_plane):
             c.start()
-            copies.append(c)
-    for c in copies:
+
+    start = 0
+    for count in join_groups:
+        pl.when(gx >= 0)(functools.partial(group, start, start + count))
+        start += count
+    for c in puts(0, depth):
         c.wait()
 
 
@@ -378,7 +401,8 @@
         in_specs=[vmem] * 11 + [anywhere],
         out_specs=(anywhere,) * 3,
         scratch_shapes=[pltpu.VMEM(block, f32)] * 5
-        + [pltpu.VMEM(msg.shape, f32), pltpu.SemaphoreType.DMA((20,))],
+        + [pltpu.VMEM(msg.shape, f32), pltpu.VMEM(half.shape, f32), pltpu.VMEM(half.shape, f32)]
+        + [pltpu.SemaphoreType.DMA((5,))],
         input_output_aliases={11: 0},
         compiler_params=params,
         cost_estimate=cost(30, 12),

time: 17.3 us -> 16.3 us (0.942)
  Pallas kernels: 6.78 us -> 5.84 us
    pallas_call x1, Pallas kernels: 2.52 us -> 1.72 us  [local(): pl.pallas_call(own_kernel, name='own_block', out_shape=(jax.ShapeDtypeStr...]
  transfers between devices with their start and end apart: 5 -> 5, of which waited for: 1 -> 1; matrix products, arithmetic and copies ran while one was open for 0% -> 0% of each run, Pallas kernels for 15% -> 11%
where the time goes in v3:
time: 16.3 us; the launch traced here: 16.2 us
  starting transfers between devices  7.5 us (46%)
  Pallas kernels  5.84 us (36%)
  waiting for transfers between devices  2.17 us (13%)
  between operations  0.71 us (4%)
    ppermute x1, starting transfers between devices, local(): late_d = lax.ppermute(late_d, both, first(mate, y_two))  3.44 us
    pallas_call x1, Pallas kernels, local(): pl.pallas_call(edges_kernel, name='edge_sums', out_shape=(pltpu.VMEM((4,)...  2.35 us
    ppermute x1, waiting for transfers between devices, local(): early_d = lax.ppermute(early_d, both, first(y_two, mate))  2.16 us
    ppermute x1, starting transfers between devices, local(): early_c = lax.ppermute(early_c, both, first(y_one, mate))  2.13 us
    ppermute x1, starting transfers between devices, local(): early_d = lax.ppermute(early_d, both, first(y_two, mate))  1.82 us
    pallas_call x1, Pallas kernels, local(): pl.pallas_call(join_kernel, name='join', out_shape=(jax.ShapeDtypeStruct(...  1.76 us
    pallas_call x1, Pallas kernels, local(): pl.pallas_call(own_kernel, name='own_block', out_shape=(jax.ShapeDtypeStr...  1.72 us
  transfers between devices with their start and end apart: 5, of which 1 were waited for; matrix products, arithmetic and copies ran while one was open for 0% of the time, Pallas kernels for 11%

profile of v3, /device:TPU:1, one launch (start us, length us, event | category | flops | bytes accessed | tf_op | source)
XLA Modules:
  0.0 16.2 jit_solution(10910211611537571146)
XLA Ops:
  0.6 2.3 %edge_sums.1 = (f32[4,16,64,128]{3,2,1,0:T(8,128)S(1)}, f32[4,2,16,128]{3,2,1,0:T(8,128)S(1)}, f32[4,2,16,128]{3,2,1,0:T(8,128)S(1)}, f32[128,128]{1,0:T(8,128)S(1)}, f32[64,128]{1,0:T(8,128)S(1)}) custom-call(f32[16,64,128]{2,1,0:T(8,128)} %u.1, f32[16,64,128]{2,1,0:T(8,128)} %v.1, f32[16,64,128]{2,1,0:T(8,128)} %w.1, f32[16,64,128]{2,1,0:T(8,128)} %p.1), custom_call_target="tpu_custom_call" | custom-call | flops 524288 | bytes 524288 | tf_op jit(solution)/shard_map/edge_sums/pallas_call | solution.py:338
  3.0 0.0 copy-start.1
  3.0 0.0 copy-start.2
  3.0 2.1 %collective-permute-start.1 = (f32[128,128]{1,0:T(8,128)S(1)}, f32[128,128]{1,0:T(8,128)S(1)}, u32[]{:S(2)}, u32[]{:S(2)}) collective-permute-start(f32[128,128]{1,0:T(8,128)S(1)} %get-tuple-element.17), channel_id=1, source_target_pairs={{0,1},{1,0},{2,3},{3,2},{4,5},{5,4},{6,7},{7,6},{8,12},{9,13},{10,... | collective-permute-start | bytes 196616 | tf_op jit(solution)/shard_map/ppermute | solution.py:348
  5.1 1.8 %collective-permute-start.2 = (f32[64,128]{1,0:T(8,128)S(1)}, f32[64,128]{1,0:T(8,128)S(1)}, u32[]{:S(2)}, u32[]{:S(2)}) collective-permute-start(f32[64,128]{1,0:T(8,128)S(1)} %get-tuple-element.18), channel_id=1, source_target_pairs={{0,3},{1,2},{2,1},{3,0},{4,7},{5,6},{6,5},{7,4},{8,12},{9,13},{10,... | collective-permute-start | bytes 98312 | tf_op jit(solution)/shard_map/ppermute | solution.py:349
  7.0 0.0 collective-permute-start
  7.0 2.2 %collective-permute-done.2.early_d = f32[64,128]{1,0:T(8,128)S(1)} collective-permute-done((f32[64,128]{1,0:T(8,128)S(1)}, f32[64,128]{1,0:T(8,128)S(1)}, u32[]{:S(2)}, u32[]{:S(2)}) %collective-permute-start.2) | collective-permute-done | bytes 32800 | tf_op jit(solution)/shard_map/ppermute | solution.py:349
  9.1 0.0 collective-permute-done.1.early_c
  9.1 3.4 %collective-permute-start.4 = (f32[64,128]{1,0:T(8,128)S(1)}, f32[64,128]{1,0:T(8,128)S(1)}, u32[]{:S(2)}, u32[]{:S(2)}) collective-permute-start(f32[64,128]{1,0:T(8,128)S(1)} %get-tuple-element.22), channel_id=1, source_target_pairs={{0,4},{1,5},{2,6},{3,7},{4,0},{5,1},{6,2},{7,3},{8,11},{9,10},{10,... | collective-permute-start | bytes 98312 | tf_op jit(solution)/shard_map/ppermute | solution.py:375
  12.6 0.0 copy-start
  12.6 0.1 collective-permute-start.3
  12.7 0.0 copy-done.1
  12.7 0.0 copy-done.2
  12.7 1.7 %own_block.1 = (f32[3,16,64,128]{3,2,1,0:T(8,128)}, f32[16,64,128]{2,1,0:T(8,128)S(1)}, f32[16,64,128]{2,1,0:T(8,128)S(1)}, f32[16,64,128]{2,1,0:T(8,128)S(1)}, ...) custom-call(f32[4,16,64,128]{3,2,1,0:T(8,128)S(1)} %get-tuple-element.19.fields, bf16[64,192]{1,0:T(8,128)(2,1)S(1)} %copy-done.2, ...), custom_call_target="tpu_custom_call" | custom-call | flops 2097152000 | bytes 6291456 | tf_op jit(solution)/shard_map/own_block/pallas_call | solution.py:377
  14.4 0.0 collective-permute-done
  14.4 0.0 collective-permute-done.4.late_d
  14.4 0.0 collective-permute-done.3.late_c
  14.5 0.0 copy-done
  14.5 1.8 %join.1 = (f32[3,16,64,128]{3,2,1,0:T(8,128)}, f32[3,16,64,128]{3,2,1,0:T(8,128)}, f32[16,64,128]{2,1,0:T(8,128)}) custom-call(f32[128,128]{1,0:T(8,128)S(1)} %bitcast.1, f32[128,128]{1,0:T(8,128)S(1)} %collective-permute-done.1.early_c, f32[64,128]{1,0:T(8,128)S(1)} %collective-permute-done.2.early_d, ...), custom_call_target="tpu_custom_call", output_to_operand_aliasing={{0}: (11, {})} | custom-call | flops 15728640 | bytes 6291456 | tf_op jit(solution)/shard_map/join/pallas_call | solution.py:393
  (2 shorter events, 0.0 us)
Async XLA Ops:
  3.0 9.7 %copy-start.1 = (bf16[4,256,256]{2,1,0:T(8,128)(2,1)S(1)}, bf16[4,256,256]{2,1,0:T(8,128)(2,1)}, u32[]{:S(2)}) copy-start(bf16[4,256,256]{2,1,0:T(8,128)(2,1)} %constant.7.clone.wy_all) | copy-start | bytes 1572868
  3.0 9.7 %copy-start.2 = (bf16[64,192]{1,0:T(8,128)(2,1)S(1)}, bf16[64,192]{1,0:T(8,128)(2,1)}, u32[]{:S(2)}) copy-start(bf16[64,192]{1,0:T(8,128)(2,1)} %constant.6.clone.wx) | copy-start | bytes 73732
  3.0 6.1 %collective-permute-start.1 = (f32[128,128]{1,0:T(8,128)S(1)}, f32[128,128]{1,0:T(8,128)S(1)}, u32[]{:S(2)}, u32[]{:S(2)}) collective-permute-start(f32[128,128]{1,0:T(8,128)S(1)} %get-tuple-element.17), channel_id=1, source_target_pairs={{0,1},{1,0},{2,3},{3,2},{4,5},{5,4},{6,7},{7,6},{8,12},{9,13},{10,... | collective-permute-start | bytes 196616 | tf_op jit(solution)/shard_map/ppermute | solution.py:348
  5.1 4.0 %collective-permute-start.2 = (f32[64,128]{1,0:T(8,128)S(1)}, f32[64,128]{1,0:T(8,128)S(1)}, u32[]{:S(2)}, u32[]{:S(2)}) collective-permute-start(f32[64,128]{1,0:T(8,128)S(1)} %get-tuple-element.18), channel_id=1, source_target_pairs={{0,3},{1,2},{2,1},{3,0},{4,7},{5,6},{6,5},{7,4},{8,12},{9,13},{10,... | collective-permute-start | bytes 98312 | tf_op jit(solution)/shard_map/ppermute | solution.py:349
  7.0 7.5 %collective-permute-start = (f32[4,2,16,128]{3,2,1,0:T(8,128)S(1)}, f32[4,2,16,128]{3,2,1,0:T(8,128)S(1)}, u32[]{:S(2)}, u32[]{:S(2)}) collective-permute-start(f32[4,2,16,128]{3,2,1,0:T(8,128)S(1)} %hold.1), channel_id=1, source_target_pairs={{0,252},{4,8},{8,4},{12,16},{16,12},{20,24},{24,20},{28,32},{32,28... | collective-permute-start | bytes 196616 | tf_op jit(solution)/shard_map/ppermute | solution.py:361
  9.1 5.3 %collective-permute-start.4 = (f32[64,128]{1,0:T(8,128)S(1)}, f32[64,128]{1,0:T(8,128)S(1)}, u32[]{:S(2)}, u32[]{:S(2)}) collective-permute-start(f32[64,128]{1,0:T(8,128)S(1)} %get-tuple-element.22), channel_id=1, source_target_pairs={{0,4},{1,5},{2,6},{3,7},{4,0},{5,1},{6,2},{7,3},{8,11},{9,10},{10,... | collective-permute-start | bytes 98312 | tf_op jit(solution)/shard_map/ppermute | solution.py:375
  12.6 1.9 %copy-start = (bf16[4,48,512]{2,1,0:T(8,128)(2,1)S(1)}, bf16[4,48,512]{2,1,0:T(8,128)(2,1)}, u32[]{:S(2)}) copy-start(bf16[4,48,512]{2,1,0:T(8,128)(2,1)} %constant.8.clone.spread_all) | copy-start | bytes 589828
  12.6 1.9 %collective-permute-start.3 = (f32[128,128]{1,0:T(8,128)S(1)}, f32[128,128]{1,0:T(8,128)S(1)}, u32[]{:S(2)}, u32[]{:S(2)}) collective-permute-start(f32[128,128]{1,0:T(8,128)S(1)} %get-tuple-element.21), channel_id=1, source_target_pairs={{0,4},{1,5},{2,6},{3,7},{4,0},{5,1},{6,2},{7,3},{8,9},{9,8},{10,11... | collective-permute-start | bytes 196616 | tf_op jit(solution)/shard_map/ppermute | solution.py:374

commit v4 on v3

--- a/solution.py
+++ b/solution.py
@@ -145,7 +145,7 @@
         early_c[...] = chip[...].reshape(early_c.shape)
 
 
-def late_kernel(fields, chip, early_c, early_d, late_c, late_d):
+def late_kernel(fields, chip, part, late_c, late_d):
     @pl.when(lax.axis_index("gx") < 2)
     def _():
         late_c[...] = chip[...].reshape(late_c.shape)
@@ -156,7 +156,7 @@
         y_messages(fields, late_c, late_d)
 
 
-def own_kernel(fields, wx, wy_all, lorentz, lz_o, vx_o, vy_o, vz_o, dv_o, lx_s, ly_s, sems):
+def own_block(fields, wx, wy_all, lorentz, lz_o, vx_o, vy_o, vz_o, dv_o, lx_s, ly_s, sems):
     _, depth, rows, lanes = fields.shape
     u, v, w, p = range(4)
     wy = wy_all.at[lax.axis_index("gy")]
@@ -208,6 +208,18 @@
     put_y.wait()
 
 
+def waiting_kernel(fields, wx, wy_all, early_c, early_d, *rest):
+    @pl.when(lax.axis_index("gx") == 1)
+    def _():
+        own_block(fields, wx, wy_all, *rest)
+
+
+def rest_kernel(fields, wx, wy_all, *rest):
+    @pl.when(lax.axis_index("gx") != 1)
+    def _():
+        own_block(fields, wx, wy_all, *rest[6:])
+
+
 def hold_kernel(message, held):
     pass
 
@@ -343,7 +355,7 @@
         out_specs=(vmem,) * 5,
         scratch_shapes=[pltpu.SemaphoreType.DMA((4 * pieces,))],
         compiler_params=params,
-        cost_estimate=cost(1, 1),
+        cost_estimate=cost(20000, 12),
     )(*(stay(x) for x in (u, v, w, p)))
     early_c = lax.ppermute(early_c, both, first(y_one, mate))
     early_d = lax.ppermute(early_d, both, first(y_two, mate))
@@ -356,38 +368,52 @@
         out_specs=vmem,
         input_output_aliases={0: 0},
         compiler_params=params,
-        cost_estimate=cost(1, 1),
+        cost_estimate=cost(20000, 12),
     )(keep(far_side))
     got_far = lax.ppermute(
         far_side, "gx", [(i, (i + 1) % ring if i % 2 else (i - 1) % ring) for i in range(ring)]
     )
 
+    parts = (jax.ShapeDtypeStruct((3,) + block, f32),) + (pltpu.VMEM(block, f32),) * 5
+    scratch = [
+        pltpu.VMEM(block, f32),
+        pltpu.VMEM(block, f32),
+        pltpu.SemaphoreType.DMA((2,)),
+    ]
+    lorentz, *part = pl.pallas_call(
+        waiting_kernel,
+        name="own_block_column_one",
+        out_shape=parts,
+        in_specs=[vmem] * 3 + [anywhere] * 2,
+        out_specs=(anywhere,) + (vmem,) * 5,
+        scratch_shapes=scratch,
+        compiler_params=params,
+        cost_estimate=cost(1, 1),
+    )(keep(fields), wx, wy, keep(early_c), keep(early_d))
+
     late_c, late_d = pl.pallas_call(
         late_kernel,
         name="y_sums",
         out_shape=(msg, half),
-        in_specs=[vmem, vmem, anywhere, anywhere],
+        in_specs=[vmem, vmem, anywhere],
         out_specs=(vmem,) * 2,
         compiler_params=params,
         cost_estimate=cost(1, 1),
-    )(*(keep(x) for x in (fields, chip, early_c, early_d)))
+    )(*(keep(x) for x in (fields, chip, part[0])))
     late_c = lax.ppermute(late_c, both, first(mate, y_one))
     late_d = lax.ppermute(late_d, both, first(mate, y_two))
 
     lorentz, *part = pl.pallas_call(
-        own_kernel,
+        rest_kernel,
         name="own_block",
-        out_shape=(jax.ShapeDtypeStruct((3,) + block, f32),) + (pltpu.VMEM(block, f32),) * 5,
-        in_specs=[vmem] * 3,
+        out_shape=parts,
+        in_specs=[vmem] * 3 + [anywhere] + [vmem] * 5,
         out_specs=(anywhere,) + (vmem,) * 5,
-        scratch_shapes=[
-            pltpu.VMEM(block, f32),
-            pltpu.VMEM(block, f32),
-            pltpu.SemaphoreType.DMA((2,)),
-        ],
-        compiler_params=params,
-        cost_estimate=cost(4000, 12),
-    )(keep(fields), wx, wy)
+        scratch_shapes=scratch,
+        input_output_aliases={i + 3: i for i in range(6)},
+        compiler_params=params,
+        cost_estimate=cost(100, 12),
+    )(keep(fields), wx, wy, lorentz, *(keep(x) for x in part))
 
     got_far = got_far.reshape(msg.shape)
     return pl.pallas_call(
@@ -405,7 +431,7 @@
         + [pltpu.SemaphoreType.DMA((5,))],
         input_output_aliases={11: 0},
         compiler_params=params,
-        cost_estimate=cost(30, 12),
+        cost_estimate=cost(10, 10),
     )(
         *(keep(x) for x in (got_far, early_c, early_d, late_c, late_d)),
         spread,

time: 16.3 us -> 15.7 us (0.963)
  starting transfers between devices: 7.5 us -> 5.81 us
  waiting for transfers between devices: 2.17 us -> 3.23 us
    ppermute x1, starting transfers between devices: 3.44 us -> 0.1 us  [local(): late_d = lax.ppermute(late_d, both, first(mate, y_two))]
    ppermute x1, starting transfers between devices: 0.11 us -> 1.76 us  [local(): late_c = lax.ppermute(late_c, both, first(mate, y_one))]
    ppermute x1, waiting for transfers between devices: 0.01 us -> 1.07 us  [local(): late_d = lax.ppermute(late_d, both, first(mate, y_two))]
    pallas_call x1 -> x2, Pallas kernels: 1.72 us -> 1.75 us  [the longest x1 1.73 us: local(): pl.pallas_call(waiting_kernel, name='own_block_column_one', out_shape=par...]
  transfers between devices with their start and end apart: 5 -> 5, of which waited for: 1 -> 2; matrix products, arithmetic and copies ran while one was open for 0% -> 0% of each run, Pallas kernels for 11% -> 11%
where the time goes in v4:
time: 15.7 us; the launch traced here: 15.6 us
  Pallas kernels  5.89 us (38%)
  starting transfers between devices  5.81 us (37%)
  waiting for transfers between devices  3.23 us (21%)
  between operations  0.68 us (4%)
    pallas_call x1, Pallas kernels, local(): pl.pallas_call(edges_kernel, name='edge_sums', out_shape=(pltpu.VMEM((4,)...  2.35 us
    ppermute x1, waiting for transfers between devices, local(): early_d = lax.ppermute(early_d, both, first(y_two, mate))  2.15 us
    ppermute x1, starting transfers between devices, local(): early_c = lax.ppermute(early_c, both, first(y_one, mate))  2.13 us
    ppermute x1, starting transfers between devices, local(): early_d = lax.ppermute(early_d, both, first(y_two, mate))  1.82 us
    pallas_call x1, Pallas kernels, local(): pl.pallas_call(join_kernel, name='join', out_shape=(jax.ShapeDtypeStruct(...  1.77 us
    ppermute x1, starting transfers between devices, local(): late_c = lax.ppermute(late_c, both, first(mate, y_one))  1.76 us
    pallas_call x1, Pallas kernels, local(): pl.pallas_call(waiting_kernel, name='own_block_column_one', out_shape=par...  1.73 us
    ppermute x1, waiting for transfers between devices, local(): late_d = lax.ppermute(late_d, both, first(mate, y_two))  1.07 us
  transfers between devices with their start and end apart: 5, of which 2 were waited for; matrix products, arithmetic and copies ran while one was open for 0% of the time, Pallas kernels for 11%

profile of v4, /device:TPU:1, one launch (start us, length us, event | category | flops | bytes accessed | tf_op | source)
XLA Modules:
  0.0 15.6 jit_solution(13779704853784068784)
XLA Ops:
  0.6 2.3 %edge_sums.1 = (f32[4,16,64,128]{3,2,1,0:T(8,128)S(1)}, f32[4,2,16,128]{3,2,1,0:T(8,128)S(1)}, f32[4,2,16,128]{3,2,1,0:T(8,128)S(1)}, f32[128,128]{1,0:T(8,128)S(1)}, f32[64,128]{1,0:T(8,128)S(1)}) custom-call(f32[16,64,128]{2,1,0:T(8,128)} %u.1, f32[16,64,128]{2,1,0:T(8,128)} %v.1, f32[16,64,128]{2,1,0:T(8,128)} %w.1, f32[16,64,128]{2,1,0:T(8,128)} %p.1), custom_call_target="tpu_custom_call" | custom-call | flops 10485760000 | bytes 6291456 | tf_op jit(solution)/shard_map/edge_sums/pallas_call | solution.py:350
  3.0 2.1 %collective-permute-start.1 = (f32[128,128]{1,0:T(8,128)S(1)}, f32[128,128]{1,0:T(8,128)S(1)}, u32[]{:S(2)}, u32[]{:S(2)}) collective-permute-start(f32[128,128]{1,0:T(8,128)S(1)} %get-tuple-element.23), channel_id=1, source_target_pairs={{0,1},{1,0},{2,3},{3,2},{4,5},{5,4},{6,7},{7,6},{8,12},{9,13},{10,... | collective-permute-start | bytes 196616 | tf_op jit(solution)/shard_map/ppermute | solution.py:360
  5.1 1.8 %collective-permute-start.2 = (f32[64,128]{1,0:T(8,128)S(1)}, f32[64,128]{1,0:T(8,128)S(1)}, u32[]{:S(2)}, u32[]{:S(2)}) collective-permute-start(f32[64,128]{1,0:T(8,128)S(1)} %get-tuple-element.24), channel_id=1, source_target_pairs={{0,3},{1,2},{2,1},{3,0},{4,7},{5,6},{6,5},{7,4},{8,12},{9,13},{10,... | collective-permute-start | bytes 98312 | tf_op jit(solution)/shard_map/ppermute | solution.py:361
  6.9 0.0 copy-start
  6.9 0.0 copy-start.2
  6.9 0.0 collective-permute-start
  6.9 2.1 %collective-permute-done.2.early_d = f32[64,128]{1,0:T(8,128)S(1)} collective-permute-done((f32[64,128]{1,0:T(8,128)S(1)}, f32[64,128]{1,0:T(8,128)S(1)}, u32[]{:S(2)}, u32[]{:S(2)}) %collective-permute-start.2) | collective-permute-done | bytes 32800 | tf_op jit(solution)/shard_map/ppermute | solution.py:361
  9.1 0.0 collective-permute-done.1.early_c
  9.1 0.0 copy-done
  9.1 0.0 copy-done.2
  9.1 1.7 %own_block_column_one.1 = (f32[3,16,64,128]{3,2,1,0:T(8,128)}, f32[16,64,128]{2,1,0:T(8,128)S(1)}, f32[16,64,128]{2,1,0:T(8,128)S(1)}, f32[16,64,128]{2,1,0:T(8,...) custom-call(f32[4,16,64,128]{3,2,1,0:T(8,128)S(1)} %get-tuple-element.25.fields, ...), custom_call_target="tpu_custom_call" | custom-call | flops 524288 | bytes 524288 | tf_op jit(solution)/shard_map/own_block_column_one/pallas_call | solution.py:383
  10.9 1.8 %collective-permute-start.3 = (f32[128,128]{1,0:T(8,128)S(1)}, f32[128,128]{1,0:T(8,128)S(1)}, u32[]{:S(2)}, u32[]{:S(2)}) collective-permute-start(f32[128,128]{1,0:T(8,128)S(1)} %get-tuple-element.28), channel_id=1, source_target_pairs={{0,4},{1,5},{2,6},{3,7},{4,0},{5,1},{6,2},{7,3},{8,9},{9,8},{10,11... | collective-permute-start | bytes 196616 | tf_op jit(solution)/shard_map/ppermute | solution.py:403
  12.6 0.1 collective-permute-start.4
  12.7 0.0 copy-start.1
  12.8 0.0 collective-permute-done
  12.8 1.1 %collective-permute-done.4.late_d = f32[64,128]{1,0:T(8,128)S(1)} collective-permute-done((f32[64,128]{1,0:T(8,128)S(1)}, f32[64,128]{1,0:T(8,128)S(1)}, u32[]{:S(2)}, u32[]{:S(2)}) %collective-permute-start.4) | collective-permute-done | bytes 32800 | tf_op jit(solution)/shard_map/ppermute | solution.py:404
  13.8 0.0 collective-permute-done.3.late_c
  13.8 0.0 copy-done.1
  13.8 1.8 %join.1 = (f32[3,16,64,128]{3,2,1,0:T(8,128)}, f32[3,16,64,128]{3,2,1,0:T(8,128)}, f32[16,64,128]{2,1,0:T(8,128)}) custom-call(f32[128,128]{1,0:T(8,128)S(1)} %bitcast.1, f32[128,128]{1,0:T(8,128)S(1)} %collective-permute-done.1.early_c, f32[64,128]{1,0:T(8,128)S(1)} %collective-permute-done.2.early_d, ...), custom_call_target="tpu_custom_call", output_to_operand_aliasing={{0}: (11, {})} | custom-call | flops 5242880 | bytes 5242880 | tf_op jit(solution)/shard_map/join/pallas_call | solution.py:419
  (3 shorter events, 0.0 us)
Async XLA Ops:
  3.0 6.1 %collective-permute-start.1 = (f32[128,128]{1,0:T(8,128)S(1)}, f32[128,128]{1,0:T(8,128)S(1)}, u32[]{:S(2)}, u32[]{:S(2)}) collective-permute-start(f32[128,128]{1,0:T(8,128)S(1)} %get-tuple-element.23), channel_id=1, source_target_pairs={{0,1},{1,0},{2,3},{3,2},{4,5},{5,4},{6,7},{7,6},{8,12},{9,13},{10,... | collective-permute-start | bytes 196616 | tf_op jit(solution)/shard_map/ppermute | solution.py:360
  5.1 4.0 %collective-permute-start.2 = (f32[64,128]{1,0:T(8,128)S(1)}, f32[64,128]{1,0:T(8,128)S(1)}, u32[]{:S(2)}, u32[]{:S(2)}) collective-permute-start(f32[64,128]{1,0:T(8,128)S(1)} %get-tuple-element.24), channel_id=1, source_target_pairs={{0,3},{1,2},{2,1},{3,0},{4,7},{5,6},{6,5},{7,4},{8,12},{9,13},{10,... | collective-permute-start | bytes 98312 | tf_op jit(solution)/shard_map/ppermute | solution.py:361
  6.9 2.2 %copy-start = (bf16[4,256,256]{2,1,0:T(8,128)(2,1)S(1)}, bf16[4,256,256]{2,1,0:T(8,128)(2,1)}, u32[]{:S(2)}) copy-start(bf16[4,256,256]{2,1,0:T(8,128)(2,1)} %constant.7.clone.wy_all) | copy-start | bytes 1572868
  6.9 2.2 %copy-start.2 = (bf16[64,192]{1,0:T(8,128)(2,1)S(1)}, bf16[64,192]{1,0:T(8,128)(2,1)}, u32[]{:S(2)}) copy-start(bf16[64,192]{1,0:T(8,128)(2,1)} %constant.6.clone.wx) | copy-start | bytes 73732
  6.9 5.8 %collective-permute-start = (f32[4,2,16,128]{3,2,1,0:T(8,128)S(1)}, f32[4,2,16,128]{3,2,1,0:T(8,128)S(1)}, u32[]{:S(2)}, u32[]{:S(2)}) collective-permute-start(f32[4,2,16,128]{3,2,1,0:T(8,128)S(1)} %hold.1), channel_id=1, source_target_pairs={{0,252},{4,8},{8,4},{12,16},{16,12},{20,24},{24,20},{28,32},{32,28... | collective-permute-start | bytes 196616 | tf_op jit(solution)/shard_map/ppermute | solution.py:373
  10.9 3.0 %collective-permute-start.3 = (f32[128,128]{1,0:T(8,128)S(1)}, f32[128,128]{1,0:T(8,128)S(1)}, u32[]{:S(2)}, u32[]{:S(2)}) collective-permute-start(f32[128,128]{1,0:T(8,128)S(1)} %get-tuple-element.28), channel_id=1, source_target_pairs={{0,4},{1,5},{2,6},{3,7},{4,0},{5,1},{6,2},{7,3},{8,9},{9,8},{10,11... | collective-permute-start | bytes 196616 | tf_op jit(solution)/shard_map/ppermute | solution.py:403
  12.6 1.2 %collective-permute-start.4 = (f32[64,128]{1,0:T(8,128)S(1)}, f32[64,128]{1,0:T(8,128)S(1)}, u32[]{:S(2)}, u32[]{:S(2)}) collective-permute-start(f32[64,128]{1,0:T(8,128)S(1)} %get-tuple-element.29), channel_id=1, source_target_pairs={{0,4},{1,5},{2,6},{3,7},{4,0},{5,1},{6,2},{7,3},{8,11},{9,10},{10,... | collective-permute-start | bytes 98312 | tf_op jit(solution)/shard_map/ppermute | solution.py:404
  12.7 1.1 %copy-start.1 = (bf16[4,48,512]{2,1,0:T(8,128)(2,1)S(1)}, bf16[4,48,512]{2,1,0:T(8,128)(2,1)}, u32[]{:S(2)}) copy-start(bf16[4,48,512]{2,1,0:T(8,128)(2,1)} %constant.8.clone.spread_all) | copy-start | bytes 589828

commit v5 on v4

--- a/solution.py
+++ b/solution.py
@@ -401,7 +401,8 @@
         cost_estimate=cost(1, 1),
     )(*(keep(x) for x in (fields, chip, part[0])))
     late_c = lax.ppermute(late_c, both, first(mate, y_one))
-    late_d = lax.ppermute(late_d, both, first(mate, y_two))
+    inner_two = lambda i, j: y_two(i, j) if 0 < j < line - 1 else mate(i, j)
+    late_d = lax.ppermute(late_d, both, first(mate, inner_two))
 
     lorentz, *part = pl.pallas_call(
         rest_kernel,

time: 15.7 us -> 15.7 us (level)
  no operation moved by 1% of the time
where the time goes in v5:
time: 15.7 us; the launch traced here: 15.6 us
  Pallas kernels  5.89 us (38%)
  starting transfers between devices  5.81 us (37%)
  waiting for transfers between devices  3.23 us (21%)
  between operations  0.68 us (4%)
    pallas_call x1, Pallas kernels, local(): pl.pallas_call(edges_kernel, name='edge_sums', out_shape=(pltpu.VMEM((4,)...  2.35 us
    ppermute x1, waiting for transfers between devices, local(): early_d = lax.ppermute(early_d, both, first(y_two, mate))  2.15 us
    ppermute x1, starting transfers between devices, local(): early_c = lax.ppermute(early_c, both, first(y_one, mate))  2.13 us
    ppermute x1, starting transfers between devices, local(): early_d = lax.ppermute(early_d, both, first(y_two, mate))  1.82 us
    pallas_call x1, Pallas kernels, local(): pl.pallas_call(join_kernel, name='join', out_shape=(jax.ShapeDtypeStruct(...  1.77 us
    ppermute x1, starting transfers between devices, local(): late_c = lax.ppermute(late_c, both, first(mate, y_one))  1.76 us
    pallas_call x1, Pallas kernels, local(): pl.pallas_call(waiting_kernel, name='own_block_column_one', out_shape=par...  1.73 us
    ppermute x1, waiting for transfers between devices, local(): late_d = lax.ppermute(late_d, both, first(mate, inner_two))  1.07 us
  transfers between devices with their start and end apart: 5, of which 2 were waited for; matrix products, arithmetic and copies ran while one was open for 0% of the time, Pallas kernels for 11%

profile of v5, /device:TPU:1, one launch (start us, length us, event | category | flops | bytes accessed | tf_op | source)
XLA Modules:
  0.0 15.6 jit_solution(10405171282580836648)
XLA Ops:
  0.6 2.3 %edge_sums.1 = (f32[4,16,64,128]{3,2,1,0:T(8,128)S(1)}, f32[4,2,16,128]{3,2,1,0:T(8,128)S(1)}, f32[4,2,16,128]{3,2,1,0:T(8,128)S(1)}, f32[128,128]{1,0:T(8,128)S(1)}, f32[64,128]{1,0:T(8,128)S(1)}) custom-call(f32[16,64,128]{2,1,0:T(8,128)} %u.1, f32[16,64,128]{2,1,0:T(8,128)} %v.1, f32[16,64,128]{2,1,0:T(8,128)} %w.1, f32[16,64,128]{2,1,0:T(8,128)} %p.1), custom_call_target="tpu_custom_call" | custom-call | flops 10485760000 | bytes 6291456 | tf_op jit(solution)/shard_map/edge_sums/pallas_call | solution.py:350
  3.0 2.1 %collective-permute-start.1 = (f32[128,128]{1,0:T(8,128)S(1)}, f32[128,128]{1,0:T(8,128)S(1)}, u32[]{:S(2)}, u32[]{:S(2)}) collective-permute-start(f32[128,128]{1,0:T(8,128)S(1)} %get-tuple-element.23), channel_id=1, source_target_pairs={{0,1},{1,0},{2,3},{3,2},{4,5},{5,4},{6,7},{7,6},{8,12},{9,13},{10,... | collective-permute-start | bytes 196616 | tf_op jit(solution)/shard_map/ppermute | solution.py:360
  5.1 1.8 %collective-permute-start.2 = (f32[64,128]{1,0:T(8,128)S(1)}, f32[64,128]{1,0:T(8,128)S(1)}, u32[]{:S(2)}, u32[]{:S(2)}) collective-permute-start(f32[64,128]{1,0:T(8,128)S(1)} %get-tuple-element.24), channel_id=1, source_target_pairs={{0,3},{1,2},{2,1},{3,0},{4,7},{5,6},{6,5},{7,4},{8,12},{9,13},{10,... | collective-permute-start | bytes 98312 | tf_op jit(solution)/shard_map/ppermute | solution.py:361
  6.9 0.0 copy-start
  6.9 0.0 copy-start.2
  6.9 0.0 collective-permute-start
  6.9 2.1 %collective-permute-done.2.early_d = f32[64,128]{1,0:T(8,128)S(1)} collective-permute-done((f32[64,128]{1,0:T(8,128)S(1)}, f32[64,128]{1,0:T(8,128)S(1)}, u32[]{:S(2)}, u32[]{:S(2)}) %collective-permute-start.2) | collective-permute-done | bytes 32800 | tf_op jit(solution)/shard_map/ppermute | solution.py:361
  9.1 0.0 collective-permute-done.1.early_c
  9.1 0.0 copy-done
  9.1 0.0 copy-done.2
  9.1 1.7 %own_block_column_one.1 = (f32[3,16,64,128]{3,2,1,0:T(8,128)}, f32[16,64,128]{2,1,0:T(8,128)S(1)}, f32[16,64,128]{2,1,0:T(8,128)S(1)}, f32[16,64,128]{2,1,0:T(8,...) custom-call(f32[4,16,64,128]{3,2,1,0:T(8,128)S(1)} %get-tuple-element.25.fields, ...), custom_call_target="tpu_custom_call" | custom-call | flops 524288 | bytes 524288 | tf_op jit(solution)/shard_map/own_block_column_one/pallas_call | solution.py:383
  10.9 1.8 %collective-permute-start.3 = (f32[128,128]{1,0:T(8,128)S(1)}, f32[128,128]{1,0:T(8,128)S(1)}, u32[]{:S(2)}, u32[]{:S(2)}) collective-permute-start(f32[128,128]{1,0:T(8,128)S(1)} %get-tuple-element.28), channel_id=1, source_target_pairs={{0,4},{1,5},{2,6},{3,7},{4,0},{5,1},{6,2},{7,3},{8,9},{9,8},{10,11... | collective-permute-start | bytes 196616 | tf_op jit(solution)/shard_map/ppermute | solution.py:403
  12.6 0.1 collective-permute-start.4
  12.7 0.0 copy-start.1
  12.8 0.0 collective-permute-done
  12.8 1.1 %collective-permute-done.4.late_d = f32[64,128]{1,0:T(8,128)S(1)} collective-permute-done((f32[64,128]{1,0:T(8,128)S(1)}, f32[64,128]{1,0:T(8,128)S(1)}, u32[]{:S(2)}, u32[]{:S(2)}) %collective-permute-start.4) | collective-permute-done | bytes 32800 | tf_op jit(solution)/shard_map/ppermute | solution.py:405
  13.8 0.0 collective-permute-done.3.late_c
  13.8 0.0 copy-done.1
  13.8 1.8 %join.1 = (f32[3,16,64,128]{3,2,1,0:T(8,128)}, f32[3,16,64,128]{3,2,1,0:T(8,128)}, f32[16,64,128]{2,1,0:T(8,128)}) custom-call(f32[128,128]{1,0:T(8,128)S(1)} %bitcast.1, f32[128,128]{1,0:T(8,128)S(1)} %collective-permute-done.1.early_c, f32[64,128]{1,0:T(8,128)S(1)} %collective-permute-done.2.early_d, ...), custom_call_target="tpu_custom_call", output_to_operand_aliasing={{0}: (11, {})} | custom-call | flops 5242880 | bytes 5242880 | tf_op jit(solution)/shard_map/join/pallas_call | solution.py:420
  (3 shorter events, 0.0 us)
Async XLA Ops:
  3.0 6.1 %collective-permute-start.1 = (f32[128,128]{1,0:T(8,128)S(1)}, f32[128,128]{1,0:T(8,128)S(1)}, u32[]{:S(2)}, u32[]{:S(2)}) collective-permute-start(f32[128,128]{1,0:T(8,128)S(1)} %get-tuple-element.23), channel_id=1, source_target_pairs={{0,1},{1,0},{2,3},{3,2},{4,5},{5,4},{6,7},{7,6},{8,12},{9,13},{10,... | collective-permute-start | bytes 196616 | tf_op jit(solution)/shard_map/ppermute | solution.py:360
  5.1 4.0 %collective-permute-start.2 = (f32[64,128]{1,0:T(8,128)S(1)}, f32[64,128]{1,0:T(8,128)S(1)}, u32[]{:S(2)}, u32[]{:S(2)}) collective-permute-start(f32[64,128]{1,0:T(8,128)S(1)} %get-tuple-element.24), channel_id=1, source_target_pairs={{0,3},{1,2},{2,1},{3,0},{4,7},{5,6},{6,5},{7,4},{8,12},{9,13},{10,... | collective-permute-start | bytes 98312 | tf_op jit(solution)/shard_map/ppermute | solution.py:361
  6.9 2.2 %copy-start = (bf16[4,256,256]{2,1,0:T(8,128)(2,1)S(1)}, bf16[4,256,256]{2,1,0:T(8,128)(2,1)}, u32[]{:S(2)}) copy-start(bf16[4,256,256]{2,1,0:T(8,128)(2,1)} %constant.7.clone.wy_all) | copy-start | bytes 1572868
  6.9 2.2 %copy-start.2 = (bf16[64,192]{1,0:T(8,128)(2,1)S(1)}, bf16[64,192]{1,0:T(8,128)(2,1)}, u32[]{:S(2)}) copy-start(bf16[64,192]{1,0:T(8,128)(2,1)} %constant.6.clone.wx) | copy-start | bytes 73732
  6.9 5.8 %collective-permute-start = (f32[4,2,16,128]{3,2,1,0:T(8,128)S(1)}, f32[4,2,16,128]{3,2,1,0:T(8,128)S(1)}, u32[]{:S(2)}, u32[]{:S(2)}) collective-permute-start(f32[4,2,16,128]{3,2,1,0:T(8,128)S(1)} %hold.1), channel_id=1, source_target_pairs={{0,252},{4,8},{8,4},{12,16},{16,12},{20,24},{24,20},{28,32},{32,28... | collective-permute-start | bytes 196616 | tf_op jit(solution)/shard_map/ppermute | solution.py:373
  10.9 3.0 %collective-permute-start.3 = (f32[128,128]{1,0:T(8,128)S(1)}, f32[128,128]{1,0:T(8,128)S(1)}, u32[]{:S(2)}, u32[]{:S(2)}) collective-permute-start(f32[128,128]{1,0:T(8,128)S(1)} %get-tuple-element.28), channel_id=1, source_target_pairs={{0,4},{1,5},{2,6},{3,7},{4,0},{5,1},{6,2},{7,3},{8,9},{9,8},{10,11... | collective-permute-start | bytes 196616 | tf_op jit(solution)/shard_map/ppermute | solution.py:403
  12.6 1.2 %collective-permute-start.4 = (f32[64,128]{1,0:T(8,128)S(1)}, f32[64,128]{1,0:T(8,128)S(1)}, u32[]{:S(2)}, u32[]{:S(2)}) collective-permute-start(f32[64,128]{1,0:T(8,128)S(1)} %get-tuple-element.29), channel_id=1, source_target_pairs={{0,4},{1,5},{2,6},{3,7},{4,0},{5,1},{6,2},{7,3},{8,12},{9,10},{10,... | collective-permute-start | bytes 98312 | tf_op jit(solution)/shard_map/ppermute | solution.py:405
  12.7 1.1 %copy-start.1 = (bf16[4,48,512]{2,1,0:T(8,128)(2,1)S(1)}, bf16[4,48,512]{2,1,0:T(8,128)(2,1)}, u32[]{:S(2)}) copy-start(bf16[4,48,512]{2,1,0:T(8,128)(2,1)} %constant.8.clone.spread_all) | copy-start | bytes 589828

commit v6 on v5

--- a/solution.py
+++ b/solution.py
@@ -126,7 +126,6 @@
             c.start()
     gx = lax.axis_index("gx")
     even_x = lax.rem(gx, 2) == 0
-    early_d[...] = jnp.zeros_like(early_d)
     for i in range(4):
         for n in range(pieces):
             copies[i][n].wait()
@@ -137,19 +136,19 @@
 
     @pl.when(gx < 2)
     def _():
-        early_c[...] = jnp.zeros_like(early_c)
         y_messages(fields, early_c, early_d)
 
     @pl.when(gx >= 2)
     def _():
-        early_c[...] = chip[...].reshape(early_c.shape)
+        early_c[...] = chip[:2].reshape(early_c.shape)
+        early_d[...] = chip[2:].reshape(early_d.shape)
 
 
 def late_kernel(fields, chip, part, late_c, late_d):
     @pl.when(lax.axis_index("gx") < 2)
     def _():
-        late_c[...] = chip[...].reshape(late_c.shape)
-        late_d[...] = jnp.zeros_like(late_d)
+        late_c[...] = chip[:2].reshape(late_c.shape)
+        late_d[...] = chip[2:].reshape(late_d.shape)
 
     @pl.when(lax.axis_index("gx") >= 2)
     def _():
@@ -253,9 +252,11 @@
     even_x = lax.rem(gx, 2) == 0
     first = gx < 2
     spread = spread_all[lax.axis_index("gy")]
-    got_c[...] = jnp.where(first, early_c[: got_c.shape[0]], late_c[: got_c.shape[0]])
+    got_c[...] = jnp.where(first, early_c[...], late_c[...])
     got_d[...] = jnp.where(first, early_d[...], late_d[...])
-    chip_s[...] = jnp.where(first, late_c[...], early_c[...])
+    middle = got_c.shape[0]
+    chip_s[:middle] = jnp.where(first, late_c[...], early_c[...])
+    chip_s[middle:] = jnp.where(first, late_d[...], early_d[...])
     i = lax.broadcasted_iota(jnp.int32, (rows, lanes), 0)
     fall_l, fall_r = power(i), power(rows - 1 - i)
     fall_chip = jnp.where(even_x, fall_r, fall_l)
@@ -350,7 +351,7 @@
     fields, chip, far_side, early_c, early_d = pl.pallas_call(
         edges_kernel,
         name="edge_sums",
-        out_shape=(pltpu.VMEM((4,) + block, f32), x_msg, x_msg, msg, half),
+        out_shape=(pltpu.VMEM((4,) + block, f32), x_msg, x_msg, half, half),
         in_specs=[anywhere] * 4,
         out_specs=(vmem,) * 5,
         scratch_shapes=[pltpu.SemaphoreType.DMA((4 * pieces,))],
@@ -394,7 +395,7 @@
     late_c, late_d = pl.pallas_call(
         late_kernel,
         name="y_sums",
-        out_shape=(msg, half),
+        out_shape=(half, half),
         in_specs=[vmem, vmem, anywhere],
         out_specs=(vmem,) * 2,
         compiler_params=params,

time: 15.7 us -> 15.7 us (level)
    ppermute x1, waiting for transfers between devices: 1.07 us -> 0.35 us  [local(): late_d = lax.ppermute(late_d, both, first(mate, inner_two))]
    ppermute x1, waiting for transfers between devices: 0.01 us -> 0.72 us  [local(): late_c = lax.ppermute(late_c, both, first(mate, y_one))]
  transfers between devices with their start and end apart: 5 -> 5, of which waited for: 2 -> 3; matrix products, arithmetic and copies ran while one was open for 0% -> 0% of each run, Pallas kernels for 11% -> 11%
where the time goes in v6:
time: 15.7 us; the launch traced here: 15.6 us
  Pallas kernels  5.86 us (37%)
  starting transfers between devices  5.83 us (37%)
  waiting for transfers between devices  3.21 us (20%)
  between operations  0.69 us (4%)
    pallas_call x1, Pallas kernels, local(): pl.pallas_call(edges_kernel, name='edge_sums', out_shape=(pltpu.VMEM((4,)...  2.35 us
    ppermute x1, waiting for transfers between devices, local(): early_d = lax.ppermute(early_d, both, first(y_two, mate))  2.14 us
    ppermute x1, starting transfers between devices, local(): early_c = lax.ppermute(early_c, both, first(y_one, mate))  2.13 us
    ppermute x1, starting transfers between devices, local(): early_d = lax.ppermute(early_d, both, first(y_two, mate))  1.82 us
    ppermute x1, starting transfers between devices, local(): late_c = lax.ppermute(late_c, both, first(mate, y_one))  1.79 us
    pallas_call x1, Pallas kernels, local(): pl.pallas_call(join_kernel, name='join', out_shape=(jax.ShapeDtypeStruct(...  1.76 us
    pallas_call x1, Pallas kernels, local(): pl.pallas_call(waiting_kernel, name='own_block_column_one', out_shape=par...  1.71 us
    ppermute x1, waiting for transfers between devices, local(): late_c = lax.ppermute(late_c, both, first(mate, y_one))  0.72 us
  transfers between devices with their start and end apart: 5, of which 3 were waited for; matrix products, arithmetic and copies ran while one was open for 0% of the time, Pallas kernels for 11%

profile of v6, /device:TPU:1, one launch (start us, length us, event | category | flops | bytes accessed | tf_op | source)
XLA Modules:
  0.0 15.6 jit_solution(2780199806656691215)
XLA Ops:
  0.6 2.3 %edge_sums.1 = (f32[4,16,64,128]{3,2,1,0:T(8,128)S(1)}, f32[4,2,16,128]{3,2,1,0:T(8,128)S(1)}, f32[4,2,16,128]{3,2,1,0:T(8,128)S(1)}, f32[64,128]{1,0:T(8,128)S(1)}, f32[64,128]{1,0:T(8,128)S(1)}) custom-call(f32[16,64,128]{2,1,0:T(8,128)} %u.1, f32[16,64,128]{2,1,0:T(8,128)} %v.1, f32[16,64,128]{2,1,0:T(8,128)} %w.1, f32[16,64,128]{2,1,0:T(8,128)} %p.1), custom_call_target="tpu_custom_call" | custom-call | flops 10485760000 | bytes 6291456 | tf_op jit(solution)/shard_map/edge_sums/pallas_call | solution.py:351
  3.0 2.1 %collective-permute-start.1 = (f32[64,128]{1,0:T(8,128)S(1)}, f32[64,128]{1,0:T(8,128)S(1)}, u32[]{:S(2)}, u32[]{:S(2)}) collective-permute-start(f32[64,128]{1,0:T(8,128)S(1)} %get-tuple-element.23), channel_id=1, source_target_pairs={{0,1},{1,0},{2,3},{3,2},{4,5},{5,4},{6,7},{7,6},{8,12},{9,13},{10,... | collective-permute-start | bytes 98312 | tf_op jit(solution)/shard_map/ppermute | solution.py:361
  5.1 1.8 %collective-permute-start.2 = (f32[64,128]{1,0:T(8,128)S(1)}, f32[64,128]{1,0:T(8,128)S(1)}, u32[]{:S(2)}, u32[]{:S(2)}) collective-permute-start(f32[64,128]{1,0:T(8,128)S(1)} %get-tuple-element.24), channel_id=1, source_target_pairs={{0,3},{1,2},{2,1},{3,0},{4,7},{5,6},{6,5},{7,4},{8,12},{9,13},{10,... | collective-permute-start | bytes 98312 | tf_op jit(solution)/shard_map/ppermute | solution.py:362
  6.9 0.0 copy-start
  6.9 0.0 copy-start.2
  6.9 0.0 collective-permute-start
  6.9 0.0 collective-permute-done.1.early_c
  7.0 2.1 %collective-permute-done.2.early_d = f32[64,128]{1,0:T(8,128)S(1)} collective-permute-done((f32[64,128]{1,0:T(8,128)S(1)}, f32[64,128]{1,0:T(8,128)S(1)}, u32[]{:S(2)}, u32[]{:S(2)}) %collective-permute-start.2) | collective-permute-done | bytes 32800 | tf_op jit(solution)/shard_map/ppermute | solution.py:362
  9.1 0.0 copy-done
  9.1 0.0 copy-done.2
  9.1 1.7 %own_block_column_one.1 = (f32[3,16,64,128]{3,2,1,0:T(8,128)}, f32[16,64,128]{2,1,0:T(8,128)S(1)}, f32[16,64,128]{2,1,0:T(8,128)S(1)}, f32[16,64,128]{2,1,0:T(8,...) custom-call(f32[4,16,64,128]{3,2,1,0:T(8,128)S(1)} %get-tuple-element.25.fields, ...), custom_call_target="tpu_custom_call" | custom-call | flops 524288 | bytes 524288 | tf_op jit(solution)/shard_map/own_block_column_one/pallas_call | solution.py:384
  10.8 1.8 %collective-permute-start.3 = (f32[64,128]{1,0:T(8,128)S(1)}, f32[64,128]{1,0:T(8,128)S(1)}, u32[]{:S(2)}, u32[]{:S(2)}) collective-permute-start(f32[64,128]{1,0:T(8,128)S(1)} %get-tuple-element.28), channel_id=1, source_target_pairs={{0,4},{1,5},{2,6},{3,7},{4,0},{5,1},{6,2},{7,3},{8,9},{9,8},{10,11... | collective-permute-start | bytes 98312 | tf_op jit(solution)/shard_map/ppermute | solution.py:404
  12.6 0.1 collective-permute-start.4
  12.7 0.0 copy-start.1
  12.8 0.0 collective-permute-done
  12.8 0.7 %collective-permute-done.3.late_c = f32[64,128]{1,0:T(8,128)S(1)} collective-permute-done((f32[64,128]{1,0:T(8,128)S(1)}, f32[64,128]{1,0:T(8,128)S(1)}, u32[]{:S(2)}, u32[]{:S(2)}) %collective-permute-start.3) | collective-permute-done | bytes 32800 | tf_op jit(solution)/shard_map/ppermute | solution.py:404
  13.5 0.3 %collective-permute-done.4.late_d = f32[64,128]{1,0:T(8,128)S(1)} collective-permute-done((f32[64,128]{1,0:T(8,128)S(1)}, f32[64,128]{1,0:T(8,128)S(1)}, u32[]{:S(2)}, u32[]{:S(2)}) %collective-permute-start.4) | collective-permute-done | bytes 32800 | tf_op jit(solution)/shard_map/ppermute | solution.py:406
  13.8 0.0 copy-done.1
  13.8 1.8 %join.1 = (f32[3,16,64,128]{3,2,1,0:T(8,128)}, f32[3,16,64,128]{3,2,1,0:T(8,128)}, f32[16,64,128]{2,1,0:T(8,128)}) custom-call(f32[128,128]{1,0:T(8,128)S(1)} %bitcast.1, f32[64,128]{1,0:T(8,128)S(1)} %collective-permute-done.1.early_c, f32[64,128]{1,0:T(8,128)S(1)} %collective-permute-done.2.early_d, ...), custom_call_target="tpu_custom_call", output_to_operand_aliasing={{0}: (11, {})} | custom-call | flops 5242880 | bytes 5242880 | tf_op jit(solution)/shard_map/join/pallas_call | solution.py:421
  (3 shorter events, 0.0 us)
Async XLA Ops:
  3.0 4.0 %collective-permute-start.1 = (f32[64,128]{1,0:T(8,128)S(1)}, f32[64,128]{1,0:T(8,128)S(1)}, u32[]{:S(2)}, u32[]{:S(2)}) collective-permute-start(f32[64,128]{1,0:T(8,128)S(1)} %get-tuple-element.23), channel_id=1, source_target_pairs={{0,1},{1,0},{2,3},{3,2},{4,5},{5,4},{6,7},{7,6},{8,12},{9,13},{10,... | collective-permute-start | bytes 98312 | tf_op jit(solution)/shard_map/ppermute | solution.py:361
  5.1 4.0 %collective-permute-start.2 = (f32[64,128]{1,0:T(8,128)S(1)}, f32[64,128]{1,0:T(8,128)S(1)}, u32[]{:S(2)}, u32[]{:S(2)}) collective-permute-start(f32[64,128]{1,0:T(8,128)S(1)} %get-tuple-element.24), channel_id=1, source_target_pairs={{0,3},{1,2},{2,1},{3,0},{4,7},{5,6},{6,5},{7,4},{8,12},{9,13},{10,... | collective-permute-start | bytes 98312 | tf_op jit(solution)/shard_map/ppermute | solution.py:362
  6.9 2.2 %copy-start = (bf16[4,256,256]{2,1,0:T(8,128)(2,1)S(1)}, bf16[4,256,256]{2,1,0:T(8,128)(2,1)}, u32[]{:S(2)}) copy-start(bf16[4,256,256]{2,1,0:T(8,128)(2,1)} %constant.7.clone.wy_all) | copy-start | bytes 1572868
  6.9 2.2 %copy-start.2 = (bf16[64,192]{1,0:T(8,128)(2,1)S(1)}, bf16[64,192]{1,0:T(8,128)(2,1)}, u32[]{:S(2)}) copy-start(bf16[64,192]{1,0:T(8,128)(2,1)} %constant.6.clone.wx) | copy-start | bytes 73732
  6.9 5.8 %collective-permute-start = (f32[4,2,16,128]{3,2,1,0:T(8,128)S(1)}, f32[4,2,16,128]{3,2,1,0:T(8,128)S(1)}, u32[]{:S(2)}, u32[]{:S(2)}) collective-permute-start(f32[4,2,16,128]{3,2,1,0:T(8,128)S(1)} %hold.1), channel_id=1, source_target_pairs={{0,252},{4,8},{8,4},{12,16},{16,12},{20,24},{24,20},{28,32},{32,28... | collective-permute-start | bytes 196616 | tf_op jit(solution)/shard_map/ppermute | solution.py:374
  10.8 2.6 %collective-permute-start.3 = (f32[64,128]{1,0:T(8,128)S(1)}, f32[64,128]{1,0:T(8,128)S(1)}, u32[]{:S(2)}, u32[]{:S(2)}) collective-permute-start(f32[64,128]{1,0:T(8,128)S(1)} %get-tuple-element.28), channel_id=1, source_target_pairs={{0,4},{1,5},{2,6},{3,7},{4,0},{5,1},{6,2},{7,3},{8,9},{9,8},{10,11... | collective-permute-start | bytes 98312 | tf_op jit(solution)/shard_map/ppermute | solution.py:404
  12.6 1.2 %collective-permute-start.4 = (f32[64,128]{1,0:T(8,128)S(1)}, f32[64,128]{1,0:T(8,128)S(1)}, u32[]{:S(2)}, u32[]{:S(2)}) collective-permute-start(f32[64,128]{1,0:T(8,128)S(1)} %get-tuple-element.29), channel_id=1, source_target_pairs={{0,4},{1,5},{2,6},{3,7},{4,0},{5,1},{6,2},{7,3},{8,12},{9,10},{10,... | collective-permute-start | bytes 98312 | tf_op jit(solution)/shard_map/ppermute | solution.py:406
  12.7 1.1 %copy-start.1 = (bf16[4,48,512]{2,1,0:T(8,128)(2,1)S(1)}, bf16[4,48,512]{2,1,0:T(8,128)(2,1)}, u32[]{:S(2)}) copy-start(bf16[4,48,512]{2,1,0:T(8,128)(2,1)} %constant.8.clone.spread_all) | copy-start | bytes 589828
